TPU v7x, 128 devices: a whole 4x4x4 slice. The times are simulated.
128 devices in a mesh: node: 16 (over x_hi, y, core), local: 8 (over z, x_lo).
Axes of the slice: x: 4 (x_hi: 2, x_lo: 2; x = x_hi * 2 + x_lo), y: 4, z: 4, core: 2. Of those that a mesh axis runs over, the one named last changes fastest.
Arguments:
- query: bfloat16 [4096, 16384], P(None, ('node', 'local')), may hold values from -6 to 6
- key_in: bfloat16 [4096, 16384], P(None, ('node', 'local')), may hold values from -6 to 6
- value_in: bfloat16 [4096, 16384], P(None, ('node', 'local')), may hold values from -6 to 6
- filters: float32 [4096, 16384], P(('node', 'local')), may hold values from -2 to 2
- skip_gain: float32 [4096], replicated, may hold values from -4 to 4
- cotangent: bfloat16 [4096, 16384], P(None, ('node', 'local')), may hold values from -6 to 6
Outputs:
- output: bfloat16 [4096, 16384], P(None, ('node', 'local'))
- grad_query: bfloat16 [4096, 16384], P(None, ('node', 'local'))
- grad_key: bfloat16 [4096, 16384], P(None, ('node', 'local'))
- grad_value: bfloat16 [4096, 16384], P(None, ('node', 'local'))
- grad_filters: float32 [4096, 16384], P(('node', 'local'))
- grad_skip: float32 [4096], P(('node', 'local'))
All inputs are finite; a program needn't handle non-finite values.
Results may differ from a plain program's by a relative error of at most 0.0053.
Values may be sent and summed in bfloat16 or wider, within the bound.
No kernel may reach another device: no remote copies, remote signals or barrier semaphores. Data moves between devices by JAX's collectives and lax.ppermute only.
A program may use at most 192 MiB of HBM per device.

v0:
```python
import functools

import jax
import jax.numpy as jnp
import numpy as np
from jax import lax
from jax.experimental import pallas as pl
from jax.experimental.pallas import tpu as pltpu
from jax.sharding import PartitionSpec as P

F32 = jnp.float32
BF16 = jnp.bfloat16
SIDE = 128
GROUP = 8


def two_terms(values):
    high = np.asarray(values, np.float32).astype(BF16)
    low = (values - high.astype(np.float64)).astype(np.float32).astype(BF16)
    return high, low


def tables():
    index = np.arange(SIDE, dtype=np.float64)
    psi = 2.0 * np.pi * index[:, None] * (index[None, :] + 0.25) / SIDE
    phi = 2.0 * np.pi * (index[:, None] + 0.25) * index[None, :] / (SIDE * SIDE)
    theta = 2.0 * np.pi * ((index[:, None] * index[None, :]) % SIDE) / SIDE
    cos_t, sin_t = np.cos(theta), np.sin(theta)
    fold = np.concatenate([np.cos(psi).T, -np.sin(psi).T], axis=0)
    fold_hi, fold_lo = two_terms(fold)
    spread_hi, spread_lo = two_terms(np.block([[cos_t, -sin_t], [sin_t, cos_t]]))
    gather_hi, gather_lo = two_terms(np.block([[cos_t, sin_t], [-sin_t, cos_t]]) / SIDE)
    unfold_hi, unfold_lo = two_terms(np.concatenate([np.cos(psi), -np.sin(psi)], axis=1) / SIDE)
    return dict(
        fold=np.concatenate([fold_hi, fold_lo], axis=1),
        fold_hi=fold_hi,
        turn_re=np.cos(phi).astype(np.float32),
        turn_im=np.sin(phi).astype(np.float32),
        spread_hi=spread_hi, spread_lo=spread_lo,
        gather_hi=gather_hi, gather_lo=gather_lo,
        unfold_hi=unfold_hi, unfold_lo=unfold_lo,
    )


def dot(lhs, rhs):
    return jnp.dot(lhs, rhs, preferred_element_type=F32)


def split_terms(values):
    high = values.astype(BF16)
    return high, (values - high.astype(F32)).astype(BF16)


def dot_rows(values, hi, lo, passes):
    high, low = split_terms(values)
    total = dot(high, hi)
    if passes >= 2:
        total = total + dot(low, hi)
    if passes >= 3:
        total = total + dot(high, lo)
    return total


def dot_cols(hi, lo, values, passes):
    high, low = split_terms(values)
    total = dot(hi, high)
    if passes >= 2:
        total = total + dot(hi, low)
    if passes >= 3:
        total = total + dot(lo, high)
    return total


def to_spectra(folded, turn_re, turn_im, spread_hi, spread_lo, passes):
    re, im = folded[:SIDE], folded[SIDE:]
    rows = []
    for s in range(2):
        sr, si = re[:, s * SIDE:(s + 1) * SIDE], im[:, s * SIDE:(s + 1) * SIDE]
        rows.append(jnp.concatenate([sr * turn_re + si * turn_im, si * turn_re - sr * turn_im], axis=1))
    return dot_rows(jnp.concatenate(rows, axis=0), spread_hi, spread_lo, passes)


def from_spectra(spectra, turn_re, turn_im, gather_hi, gather_lo, unfold_hi, unfold_lo, passes_g, passes_u):
    part = dot_rows(spectra, gather_hi, gather_lo, passes_g)
    cols = []
    for s in range(2):
        pr, pi = part[s * SIDE:(s + 1) * SIDE, :SIDE], part[s * SIDE:(s + 1) * SIDE, SIDE:]
        cols.append(jnp.concatenate([pr * turn_re - pi * turn_im, pi * turn_re + pr * turn_im], axis=0))
    return dot_cols(unfold_hi, unfold_lo, jnp.concatenate(cols, axis=1), passes_u)


def filter_kernel(fil, fold, fold_hi, turn_re, turn_im, spread_hi, spread_lo, spec, stage):
    for a in range(SIDE):
        stage[a * GROUP:(a + 1) * GROUP, :] = fil[:, a * SIDE:(a + 1) * SIDE]
    tr, ti = turn_re[...], turn_im[...]
    for c in range(0, GROUP, 2):
        pair = jnp.concatenate([stage[pl.ds(c, SIDE, stride=GROUP), :], stage[pl.ds(c + 1, SIDE, stride=GROUP), :]], axis=1)
        high, low = split_terms(pair)
        folded = dot(fold[...], jnp.concatenate([high, high], axis=0)) + dot(fold_hi[...], low)
        out = to_spectra(folded, tr, ti, spread_hi[...], spread_lo[...], 3)
        spec[0, c] = out[:SIDE]
        spec[0, c + 1] = out[SIDE:]


def signal_kernel(passes, got, fil, fold, turn_re, turn_im, spread_hi, spread_lo, gather_hi, gather_lo, unfold_hi, unfold_lo,
                  send, cross, skip, stage, result):
    rows = 2 * GROUP
    stage[...] = got[...].astype(F32).reshape(SIDE * rows, SIDE)
    tr, ti = turn_re[...], turn_im[...]
    for c in range(GROUP):
        mix = stage[pl.ds(c, SIDE, stride=rows), :]
        wgt = stage[pl.ds(c + GROUP, SIDE, stride=rows), :]
        skip[c:c + 1, :] = jnp.sum(mix * wgt, axis=0, keepdims=True)
        pair = jnp.concatenate([mix, wgt], axis=1).astype(BF16)
        folded = dot(fold[...], jnp.concatenate([pair, pair], axis=0))
        both = to_spectra(folded, tr, ti, spread_hi[...], spread_lo[...], passes[0])
        mr, mi = both[:SIDE, :SIDE], both[:SIDE, SIDE:]
        wr, wi = both[SIDE:, :SIDE], both[SIDE:, SIDE:]
        fr, fi = fil[0, c, :, :SIDE], fil[0, c, :, SIDE:]
        cross[0, c, :, :SIDE] = wr * mr + wi * mi
        cross[0, c, :, SIDE:] = wi * mr - wr * mi
        prod = jnp.concatenate([
            jnp.concatenate([fr * mr - fi * mi, fr * mi + fi * mr], axis=1),
            jnp.concatenate([fr * wr + fi * wi, fr * wi - fi * wr], axis=1),
        ], axis=0)
        back = from_spectra(prod, tr, ti, gather_hi[...], gather_lo[...], unfold_hi[...], unfold_lo[...], passes[1], passes[2])
        result[pl.ds(c, SIDE, stride=rows), :] = back[:, :SIDE]
        result[pl.ds(c + GROUP, SIDE, stride=rows), :] = back[:, SIDE:]
    send[...] = result[...].reshape(SIDE, rows, SIDE).astype(BF16)


def grad_kernel(scale, cross, turn_re, turn_im, gather_hi, gather_lo, unfold_hi, unfold_lo, out, stage):
    tr, ti = turn_re[...], turn_im[...]
    for c in range(0, GROUP, 2):
        pair = jnp.concatenate([cross[0, c], cross[0, c + 1]], axis=0)
        back = from_spectra(pair, tr, ti, gather_hi[...], gather_lo[...], unfold_hi[...], unfold_lo[...], 3, 3) * scale
        stage[pl.ds(c, SIDE, stride=GROUP), :] = back[:, :SIDE]
        stage[pl.ds(c + 1, SIDE, stride=GROUP), :] = back[:, SIDE:]
    for a in range(SIDE):
        out[:, a * SIDE:(a + 1) * SIDE] = stage[a * GROUP:(a + 1) * GROUP, :]


def whole(array):
    return pl.BlockSpec(array.shape, lambda g: (0,) * array.ndim)


PARAMS = pltpu.CompilerParams(vmem_limit_bytes=48 * 1024 * 1024)


def cost(rows, moved):
    return pl.CostEstimate(flops=2 * rows * 256 * 256, bytes_accessed=moved, transcendentals=0)


def filter_spectra(filters, tab):
    channels, seq = filters.shape
    groups = channels // GROUP
    ops = [tab[k] for k in ("fold", "fold_hi", "turn_re", "turn_im", "spread_hi", "spread_lo")]
    return pl.pallas_call(
        filter_kernel,
        grid=(groups,),
        in_specs=[pl.BlockSpec((GROUP, seq), lambda g: (g, 0))] + [whole(o) for o in ops],
        out_specs=pl.BlockSpec((1, GROUP, SIDE, 2 * SIDE), lambda g: (g, 0, 0, 0)),
        out_shape=jax.ShapeDtypeStruct((groups, GROUP, SIDE, 2 * SIDE), F32),
        scratch_shapes=[pltpu.VMEM((SIDE * GROUP, SIDE), F32)],
        compiler_params=PARAMS,
        cost_estimate=cost(channels * 5 * SIDE, 6 * channels * seq * 2),
        name="filter_spectra",
    )(filters, *ops)


def convolve(got, spec, tab, passes):
    groups = spec.shape[0]
    channels = groups * GROUP
    ops = [tab[k] for k in ("fold", "turn_re", "turn_im", "spread_hi", "spread_lo", "gather_hi", "gather_lo", "unfold_hi", "unfold_lo")]
    rows = 2 * GROUP
    return pl.pallas_call(
        functools.partial(signal_kernel, passes),
        grid=(groups,),
        in_specs=[pl.BlockSpec((SIDE, rows, SIDE), lambda g: (0, g, 0)),
                  pl.BlockSpec((1, GROUP, SIDE, 2 * SIDE), lambda g: (g, 0, 0, 0))] + [whole(o) for o in ops],
        out_specs=[pl.BlockSpec((SIDE, rows, SIDE), lambda g: (0, g, 0)),
                   pl.BlockSpec((1, GROUP, SIDE, 2 * SIDE), lambda g: (g, 0, 0, 0)),
                   pl.BlockSpec((GROUP, SIDE), lambda g: (g, 0))],
        out_shape=[jax.ShapeDtypeStruct((SIDE, 2 * channels, SIDE), BF16),
                   jax.ShapeDtypeStruct(spec.shape, F32),
                   jax.ShapeDtypeStruct((channels, SIDE), F32)],
        scratch_shapes=[pltpu.VMEM((SIDE * rows, SIDE), F32), pltpu.VMEM((SIDE * rows, SIDE), F32)],
        compiler_params=PARAMS,
        cost_estimate=cost(channels * 17 * SIDE, 12 * channels * SIDE * SIDE),
        name="convolve",
    )(got, spec, *ops)


def filter_gradient(cross, tab, scale):
    groups = cross.shape[0]
    channels = groups * GROUP
    ops = [tab[k] for k in ("turn_re", "turn_im", "gather_hi", "gather_lo", "unfold_hi", "unfold_lo")]
    return pl.pallas_call(
        functools.partial(grad_kernel, scale),
        grid=(groups,),
        in_specs=[pl.BlockSpec((1, GROUP, SIDE, 2 * SIDE), lambda g: (g, 0, 0, 0))] + [whole(o) for o in ops],
        out_specs=pl.BlockSpec((GROUP, SIDE * SIDE), lambda g: (g, 0)),
        out_shape=jax.ShapeDtypeStruct((channels, SIDE * SIDE), F32),
        scratch_shapes=[pltpu.VMEM((SIDE * GROUP, SIDE), F32)],
        compiler_params=PARAMS,
        cost_estimate=cost(channels * 5 * SIDE, 12 * channels * SIDE * SIDE),
        name="filter_gradient",
    )(cross, *ops)


def interleave(first, second):
    parts = [x.reshape(SIDE, -1, GROUP, SIDE) for x in (first, second)]
    return jnp.stack(parts, axis=2).reshape(SIDE, -1, SIDE)


def separate(both):
    parts = both.reshape(SIDE, -1, 2, GROUP, SIDE)
    return parts[:, :, 0].reshape(-1, SIDE), parts[:, :, 1].reshape(-1, SIDE)


def exchange(blocks):
    return lax.all_to_all(blocks, ("node", "local"), split_axis=0, concat_axis=0, tiled=True)


def local(query, key_in, value_in, filters, skip_gain, cotangent):
    tab = tables()
    scale = float(filters.shape[1]) ** -0.5
    mixed = (key_in.astype(F32) * value_in.astype(F32)).astype(BF16)
    weighted = (cotangent.astype(F32) * query.astype(F32)).astype(BF16)
    got = exchange(interleave(mixed, weighted))
    spec = filter_spectra(filters, tab)
    send, cross, skip = convolve(got, spec, tab, (3, 3, 3))
    conv, back = separate(exchange(send))
    grad_filters = filter_gradient(cross, tab, scale)
    grad_skip = jnp.sum(skip, axis=1) * scale
    gain = skip_gain[:, None]
    inner = conv.astype(F32) + gain * mixed.astype(F32)
    output = (query.astype(F32) * inner).astype(BF16)
    grad_query = (cotangent.astype(F32) * inner).astype(BF16)
    dmixed = back.astype(F32) + gain * weighted.astype(F32)
    grad_key = (dmixed * value_in.astype(F32)).astype(BF16)
    grad_value = (dmixed * key_in.astype(F32)).astype(BF16)
    return (output, grad_query, grad_key, grad_value, grad_filters, grad_skip)


def solution(mesh):
    tokens = P(None, ("node", "local"))
    return jax.shard_map(
        local,
        mesh=mesh,
        in_specs=(tokens, tokens, tokens, P(("node", "local"), None), P(), tokens),
        out_specs=(tokens, tokens, tokens, tokens, P(("node", "local"), None), P(("node", "local"))),
        check_vma=False,
    )
```

profile of v0, /device:TPU:0, one launch (start us, length us, event | category | flops | bytes accessed | tf_op | source)
XLA Modules:
  0.0 113.3 jit_solution(6019110964996692925)
XLA Ops:
  0.6 2.7 %fusion.2 = (bf16[4096,128]{1,0:T(8,128)(2,1)S(1)}, bf16[4096,128]{1,0:T(8,128)(2,1)S(1)}) fusion(bf16[4096,128]{1,0:T(8,128)(2,1)} %param.18, bf16[4096,128]{1,0:T(8,128)(2,1)} %param.17, bf16[4096,128]{1,0:T(8,128)(2,1)} %param.16, bf16[4096,128]{1,0:T(8,128)(2,1)} %param.21), kind=kLoop, calls=%fused_computation.8 | loop fusion | flops 4194304 | bytes 6291456 | tf_op jit(solution)/shard_map/convert_element_type | solution.py:228
  3.4 0.0 copy-start.12
  3.4 0.0 copy-start.14
  3.4 1.9 %pad_maximum_fusion = bf16[128,4,2,8,128]{4,3,2,1,0:T(8,128)(2,1)} fusion(bf16[128,4,1,8,128]{4,3,2,1,0:T(8,128)(2,1)S(1)} %bitcast.17, bf16[128,4,1,8,128]{4,3,2,1,0:T(8,128)(2,1)S(1)} %bitcast.16), kind=kLoop, calls=%fused_computation.12 | loop fusion | flops 1048576 | bytes 4194304 | tf_op jit(solution)/shard_map/stack | solution.py:213
  5.3 0.1 copy-done.14
  5.4 0.0 copy-start.7
  5.4 0.0 copy-start.10
  5.4 11.1 %all-to-all-start = ((bf16[128,64,128]{2,1,0:T(8,128)(2,1)}), bf16[128,64,128]{2,1,0:T(8,128)(2,1)S(1)}, u32[]{:S(2)}, u32[]{:S(2)}) async-start(bf16[128,64,128]{2,1,0:T(8,128)(2,1)} %bitcast.19), calls=%async_computation | async-start | bytes 4194304 | tf_op jit(solution)/shard_map/all_to_all | solution.py:222
  16.6 0.0 copy-done.3
  16.6 0.0 copy-done.4
  16.6 0.0 copy-done.5
  16.6 0.0 copy-done.6
  16.6 0.0 copy-done.7
  16.6 0.0 copy-done.10
  16.6 0.0 copy-start
  16.6 1.6 %copy-done = f32[32,16384]{1,0:T(8,128)S(1)} copy-done((f32[32,16384]{1,0:T(8,128)S(1)}, f32[32,16384]{1,0:T(8,128)}, u32[]{:S(2)}) %copy-start) | copy-done | bytes 2097176
  18.2 6.7 %filter_spectra.1.fil = f32[4,8,128,256]{3,2,1,0:T(8,128)} custom-call(f32[32,16384]{1,0:T(8,128)S(1)} %copy-done, bf16[256,256]{1,0:T(8,128)(2,1)S(1)} %copy-done.5, bf16[256,128]{1,0:T(8,128)(2,1)S(1)} %copy-done.10, f32[128,128]{1,0:T(8,128)S(1)} %copy-done.7, f32[128,128]{1,0:T(8,128)S(1)} %copy-done.6, bf16[256,256]{1,0:T(8,128)(2,1)S(1)} %copy-done.4, ...), custom_call_target="tpu_custom_call" | custom-call | flops 2684354560 | bytes 6291456 | tf_op jit(solution)/shard_map/filter_spectra/pallas_call | solution.py:158
  25.0 21.5 %all-to-all-done.got = bf16[128,64,128]{2,1,0:T(8,128)(2,1)S(1)} async-done(((bf16[128,64,128]{2,1,0:T(8,128)(2,1)}), bf16[128,64,128]{2,1,0:T(8,128)(2,1)S(1)}, u32[]{:S(2)}, u32[]{:S(2)}) %all-to-all-start) | async-done | bytes 2097184 | tf_op jit(solution)/shard_map/all_to_all | solution.py:222
  46.5 0.0 copy-done.8
  46.5 25.7 %convolve.1 = (bf16[128,64,128]{2,1,0:T(8,128)(2,1)}, f32[4,8,128,256]{3,2,1,0:T(8,128)}, f32[32,128]{1,0:T(8,128)S(1)}) custom-call(bf16[128,64,128]{2,1,0:T(8,128)(2,1)S(1)} %all-to-all-done.got, f32[4,8,128,256]{3,2,1,0:T(8,128)} %filter_spectra.1.fil, bf16[256,256]{1,0:T(8,128)(2,1)S(1)} %copy-done.5, f32[128,128]{1,0:T(8,128)S(1)} %copy-done.7, ...), custom_call_target="tpu_custom_call" | custom-call | flops 9126805504 | bytes 6291456 | tf_op jit(solution)/shard_map/convolve/pallas_call | solution.py:176
  72.2 4.9 %all-to-all-start.1 = ((bf16[128,64,128]{2,1,0:T(8,128)(2,1)}), bf16[128,64,128]{2,1,0:T(8,128)(2,1)S(1)}, u32[]{:S(2)}, u32[]{:S(2)}) async-start(bf16[128,64,128]{2,1,0:T(8,128)(2,1)} %get-tuple-element.9), calls=%async_computation.1 | async-start | bytes 4194304 | tf_op jit(solution)/shard_map/all_to_all | solution.py:222
  77.1 0.1 reduce_sum.9
  77.2 0.5 broadcast_multiply_fusion
  77.7 2.2 %copy-done.11 = f32[4,8,128,256]{3,2,1,0:T(8,128)S(1)} copy-done((f32[4,8,128,256]{3,2,1,0:T(8,128)S(1)}, f32[4,8,128,256]{3,2,1,0:T(8,128)}, u32[]{:S(2)}) %copy-start.11) | copy-done | bytes 4194328
  79.9 8.7 %filter_gradient.1 = f32[32,16384]{1,0:T(8,128)} custom-call(f32[4,8,128,256]{3,2,1,0:T(8,128)S(1)} %copy-done.11, f32[128,128]{1,0:T(8,128)S(1)} %copy-done.7, f32[128,128]{1,0:T(8,128)S(1)} %copy-done.6, bf16[256,256]{1,0:T(8,128)(2,1)S(1)} %copy-done.2, bf16[256,256]{1,0:T(8,128)(2,1)S(1)} %copy-done.1, bf16[128,256]{1,0:T(8,128)(2,1)S(1)} %copy-done.9, ...), custom_call_target="tpu_custom_call" | custom-call | flops 2684354560 | bytes 6291456 | tf_op jit(solution)/shard_map/filter_gradient/pallas_call | solution.py:198
  88.6 18.5 %all-to-all-done.1 = bf16[128,64,128]{2,1,0:T(8,128)(2,1)S(1)} async-done(((bf16[128,64,128]{2,1,0:T(8,128)(2,1)}), bf16[128,64,128]{2,1,0:T(8,128)(2,1)S(1)}, u32[]{:S(2)}, u32[]{:S(2)}) %all-to-all-start.1) | async-done | bytes 2097184 | tf_op jit(solution)/shard_map/all_to_all | solution.py:222
  107.0 0.4 fusion.6
  107.4 0.8 copy-done.13
  108.2 0.3 copy-done.15
  108.6 0.3 copy-done.16
  108.9 0.3 copy-done.17
  109.2 4.1 %fusion.1 = (bf16[4096,128]{1,0:T(8,128)(2,1)}, bf16[4096,128]{1,0:T(8,128)(2,1)}, bf16[4096,128]{1,0:T(8,128)(2,1)}, bf16[4096,128]{1,0:T(8,128)(2,1)}) fusion(bf16[4096,128]{1,0:T(8,128)(2,1)S(1)} %copy-done.16, bf16[4096,128]{1,0:T(8,128)(2,1)S(1)} %copy-done.15, bf16[128,4,1,8,128]{4,3,2,1,0:T(8,128)(2,1)S(1)} %get-tuple-element.16, ...), kind=kLoop, calls=%fused_computation.7 | loop fusion | flops 10485760 | bytes 12599296 | tf_op jit(solution)/shard_map/convert_element_type | solution.py:242
  (19 shorter events, 0.0 us)
Async XLA Ops:
  3.4 1.9 %copy-start.12 = (bf16[4096,128]{1,0:T(8,128)(2,1)}, bf16[4096,128]{1,0:T(8,128)(2,1)S(1)}, u32[]{:S(2)}) copy-start(bf16[4096,128]{1,0:T(8,128)(2,1)S(1)} %get-tuple-element.20) | copy-start | bytes 3145732
  3.4 2.0 %copy-start.14 = (bf16[4096,128]{1,0:T(8,128)(2,1)}, bf16[4096,128]{1,0:T(8,128)(2,1)S(1)}, u32[]{:S(2)}) copy-start(bf16[4096,128]{1,0:T(8,128)(2,1)S(1)} %get-tuple-element.21) | copy-start | bytes 3145732
  5.4 11.2 %copy-start.3 = (bf16[256,256]{1,0:T(8,128)(2,1)S(1)}, bf16[256,256]{1,0:T(8,128)(2,1)}, u32[]{:S(2)}) copy-start(bf16[256,256]{1,0:T(8,128)(2,1)} %constant.29.clone.spread_lo) | copy-start | bytes 393220
  5.4 11.2 %copy-start.4 = (bf16[256,256]{1,0:T(8,128)(2,1)S(1)}, bf16[256,256]{1,0:T(8,128)(2,1)}, u32[]{:S(2)}) copy-start(bf16[256,256]{1,0:T(8,128)(2,1)} %constant.28.clone.spread_hi) | copy-start | bytes 393220
  5.4 11.2 %copy-start.5 = (bf16[256,256]{1,0:T(8,128)(2,1)S(1)}, bf16[256,256]{1,0:T(8,128)(2,1)}, u32[]{:S(2)}) copy-start(bf16[256,256]{1,0:T(8,128)(2,1)} %constant.24.clone.fold) | copy-start | bytes 393220
  5.4 11.2 %copy-start.6 = (f32[128,128]{1,0:T(8,128)S(1)}, f32[128,128]{1,0:T(8,128)}, u32[]{:S(2)}) copy-start(f32[128,128]{1,0:T(8,128)} %constant.27.clone.turn_im) | copy-start | bytes 196612
  5.4 11.2 %copy-start.7 = (f32[128,128]{1,0:T(8,128)S(1)}, f32[128,128]{1,0:T(8,128)}, u32[]{:S(2)}) copy-start(f32[128,128]{1,0:T(8,128)} %constant.26.clone.turn_re) | copy-start | bytes 196612
  5.4 11.2 %copy-start.10 = (bf16[256,128]{1,0:T(8,128)(2,1)S(1)}, bf16[256,128]{1,0:T(8,128)(2,1)}, u32[]{:S(2)}) copy-start(bf16[256,128]{1,0:T(8,128)(2,1)} %constant.25.clone.fold_hi) | copy-start | bytes 196612
  5.4 41.1 %all-to-all-start = ((bf16[128,64,128]{2,1,0:T(8,128)(2,1)}), bf16[128,64,128]{2,1,0:T(8,128)(2,1)S(1)}, u32[]{:S(2)}, u32[]{:S(2)}) async-start(bf16[128,64,128]{2,1,0:T(8,128)(2,1)} %bitcast.19), calls=%async_computation | async-start | bytes 4194304 | tf_op jit(solution)/shard_map/all_to_all | solution.py:222
  16.6 1.6 %copy-start = (f32[32,16384]{1,0:T(8,128)S(1)}, f32[32,16384]{1,0:T(8,128)}, u32[]{:S(2)}) copy-start(f32[32,16384]{1,0:T(8,128)} %fil.1) | copy-start | bytes 6291460
  18.2 28.3 %copy-start.1 = (bf16[256,256]{1,0:T(8,128)(2,1)S(1)}, bf16[256,256]{1,0:T(8,128)(2,1)}, u32[]{:S(2)}) copy-start(bf16[256,256]{1,0:T(8,128)(2,1)} %constant.31.clone.gather_lo) | copy-start | bytes 393220
  18.2 28.3 %copy-start.2 = (bf16[256,256]{1,0:T(8,128)(2,1)S(1)}, bf16[256,256]{1,0:T(8,128)(2,1)}, u32[]{:S(2)}) copy-start(bf16[256,256]{1,0:T(8,128)(2,1)} %constant.30.clone.gather_hi) | copy-start | bytes 393220
  18.2 28.3 %copy-start.8 = (bf16[128,256]{1,0:T(8,128)(2,1)S(1)}, bf16[128,256]{1,0:T(8,128)(2,1)}, u32[]{:S(2)}) copy-start(bf16[128,256]{1,0:T(8,128)(2,1)} %constant.33.clone.unfold_lo) | copy-start | bytes 196612
  18.2 28.3 %copy-start.9 = (bf16[128,256]{1,0:T(8,128)(2,1)S(1)}, bf16[128,256]{1,0:T(8,128)(2,1)}, u32[]{:S(2)}) copy-start(bf16[128,256]{1,0:T(8,128)(2,1)} %constant.32.clone.unfold_hi) | copy-start | bytes 196612
  72.2 34.8 %all-to-all-start.1 = ((bf16[128,64,128]{2,1,0:T(8,128)(2,1)}), bf16[128,64,128]{2,1,0:T(8,128)(2,1)S(1)}, u32[]{:S(2)}, u32[]{:S(2)}) async-start(bf16[128,64,128]{2,1,0:T(8,128)(2,1)} %get-tuple-element.9), calls=%async_computation.1 | async-start | bytes 4194304 | tf_op jit(solution)/shard_map/all_to_all | solution.py:222
  77.7 2.2 %copy-start.11 = (f32[4,8,128,256]{3,2,1,0:T(8,128)S(1)}, f32[4,8,128,256]{3,2,1,0:T(8,128)}, u32[]{:S(2)}) copy-start(f32[4,8,128,256]{3,2,1,0:T(8,128)} %get-tuple-element.10.cross) | copy-start | bytes 12582916
  79.9 27.5 %copy-start.18 = (f32[4096]{0:T(1024)S(1)}, f32[4096]{0:T(1024)}, u32[]{:S(2)}) copy-start(f32[4096]{0:T(1024)} %param.20) | copy-start | bytes 49156
  107.0 1.2 %copy-start.13 = (bf16[4096,128]{1,0:T(8,128)(2,1)S(1)}, bf16[4096,128]{1,0:T(8,128)(2,1)}, u32[]{:S(2)}) copy-start(bf16[4096,128]{1,0:T(8,128)(2,1)} %copy-done.12) | copy-start | bytes 3145732
  107.0 1.5 %copy-start.15 = (bf16[4096,128]{1,0:T(8,128)(2,1)S(1)}, bf16[4096,128]{1,0:T(8,128)(2,1)}, u32[]{:S(2)}) copy-start(bf16[4096,128]{1,0:T(8,128)(2,1)} %copy-done.14) | copy-start | bytes 3145732
  107.0 1.9 %copy-start.16 = (bf16[4096,128]{1,0:T(8,128)(2,1)S(1)}, bf16[4096,128]{1,0:T(8,128)(2,1)}, u32[]{:S(2)}) copy-start(bf16[4096,128]{1,0:T(8,128)(2,1)} %param.17) | copy-start | bytes 3145732
  107.0 2.2 %copy-start.17 = (bf16[4096,128]{1,0:T(8,128)(2,1)S(1)}, bf16[4096,128]{1,0:T(8,128)(2,1)}, u32[]{:S(2)}) copy-start(bf16[4096,128]{1,0:T(8,128)(2,1)} %param.18) | copy-start | bytes 3145732
where the time goes:
time: 114 us; the launch traced here: 113 us
  Pallas kernels  41.1 us (36%)
  waiting for transfers between devices  40 us (35%)
  starting transfers between devices  16 us (14%)
  other arithmetic  9.36 us (8%)
  local copies, waits for them, and re-layouts  6.06 us (5%)
    all_to_all x2, waiting for transfers between devices, exchange(): lax.all_to_all(blocks, ('node', 'local'), split_axis=0, concat_axis=0, ti...  40 us
    pallas_call x1, Pallas kernels, convolve(): pl.pallas_call(functools.partial(signal_kernel, passes), grid=(groups,),...  25.7 us
    all_to_all x2, starting transfers between devices, exchange(): lax.all_to_all(blocks, ('node', 'local'), split_axis=0, concat_axis=0, ti...  16 us
    pallas_call x1, Pallas kernels, filter_gradient(): pl.pallas_call(functools.partial(grad_kernel, scale), grid=(groups,), in_...  8.66 us
    pallas_call x1, Pallas kernels, filter_spectra(): pl.pallas_call(filter_kernel, grid=(groups,), in_specs=[pl.BlockSpec((GRO...  6.73 us
    unnamed x38, local copies, waits for them, and re-layouts  5.69 us
    convert_element_type x1, other arithmetic, local(): grad_value = (dmixed * key_in.astype(F32)).astype(BF16)  4.11 us
    convert_element_type x1, other arithmetic, local(): mixed = (key_in.astype(F32) * value_in.astype(F32)).astype(BF16)  2.72 us
  transfers between devices with their start and end apart: 2, of which 2 were waited for; matrix products, arithmetic and copies ran while one was open for 1% of the time, Pallas kernels for 14%

commit v1 on v0

v1 whole, which is shorter than its diff:
```python
import functools

import jax
import jax.numpy as jnp
import numpy as np
from jax import lax
from jax.experimental import pallas as pl
from jax.experimental.pallas import tpu as pltpu
from jax.sharding import PartitionSpec as P

F32 = jnp.float32
BF16 = jnp.bfloat16
SIDE = 128
GROUP = 8
OCTET = 8


def two_terms(values):
    high = np.asarray(values, np.float32).astype(BF16)
    low = (values - high.astype(np.float64)).astype(np.float32).astype(BF16)
    return high, low


def tables():
    index = np.arange(SIDE, dtype=np.float64)
    psi = 2.0 * np.pi * index[:, None] * (index[None, :] + 0.25) / SIDE
    phi = 2.0 * np.pi * (index[:, None] + 0.25) * index[None, :] / (SIDE * SIDE)
    theta = 2.0 * np.pi * ((index[:, None] * index[None, :]) % SIDE) / SIDE
    cos_t, sin_t = np.cos(theta), np.sin(theta)
    fold = np.concatenate([np.cos(psi).T, -np.sin(psi).T], axis=0)
    fold_hi, fold_lo = two_terms(fold)
    spread_hi, spread_lo = two_terms(np.block([[cos_t, -sin_t], [sin_t, cos_t]]))
    gather_hi, gather_lo = two_terms(np.block([[cos_t, sin_t], [-sin_t, cos_t]]) / SIDE)
    unfold_hi, unfold_lo = two_terms(np.concatenate([np.cos(psi), -np.sin(psi)], axis=1) / SIDE)
    return dict(
        fold=np.concatenate([fold_hi, fold_lo], axis=1),
        fold_hi=fold_hi,
        turn_re=np.cos(phi).astype(np.float32),
        turn_im=np.sin(phi).astype(np.float32),
        spread_hi=spread_hi, spread_lo=spread_lo,
        gather_hi=gather_hi, gather_lo=gather_lo,
        unfold_hi=unfold_hi, unfold_lo=unfold_lo,
    )


def dot(lhs, rhs):
    return jnp.dot(lhs, rhs, preferred_element_type=F32)


def join(parts, axis):
    return jnp.concatenate(parts, axis=axis)


def fold_pair(pair, exact, fold, fold_hi):
    high = pair.astype(BF16)
    folded = dot(fold[...], join([high, high], 0))
    if not exact:
        folded = folded + dot(fold_hi[...], (pair - high.astype(F32)).astype(BF16))
    return folded


def turn_folded(folded, cos_ref, sin_ref):
    turn_re, turn_im = cos_ref[...], sin_ref[...]
    rows = []
    for s in range(2):
        re, im = folded[:SIDE, s * SIDE:(s + 1) * SIDE], folded[SIDE:, s * SIDE:(s + 1) * SIDE]
        rows.append(join([re * turn_re + im * turn_im, im * turn_re - re * turn_im], 1))
    return join(rows, 0)


def turn_back(part, cos_ref, sin_ref):
    turn_re, turn_im = cos_ref[...], sin_ref[...]
    cols = []
    for s in range(2):
        re, im = part[s * SIDE:(s + 1) * SIDE, :SIDE], part[s * SIDE:(s + 1) * SIDE, SIDE:]
        cols.append(join([re * turn_re - im * turn_im, im * turn_re + re * turn_im], 0))
    return join(cols, 1)


def keep(store, c, values, passes):
    rows = pl.ds(c * 2 * SIDE, 2 * SIDE)
    high = values.astype(BF16)
    store[0, rows, :] = high
    if passes % 2 == 1 and passes > 1:
        store[1, rows, :] = (values - high.astype(F32)).astype(BF16)


def rows_times(store, c, hi, lo, passes):
    rows = pl.ds(c * 2 * SIDE, 2 * SIDE)
    high = store[0, rows, :]
    total = dot(high, hi[...])
    if passes >= 2:
        total = total + dot(high, lo[...])
    if passes >= 3:
        total = total + dot(store[1, rows, :], hi[...])
    return total


def times_rows(hi, lo, store, c, passes):
    rows = pl.ds(c * 2 * SIDE, 2 * SIDE)
    high = store[0, rows, :]
    total = dot(hi[...], high)
    if passes >= 2:
        total = total + dot(lo[...], high)
    if passes >= 3:
        total = total + dot(hi[...], store[1, rows, :])
    return total


def filter_kernel(fil, fold, fold_hi, turn_re, turn_im, spread_hi, spread_lo, spec, stage, turned):
    for a in range(SIDE):
        stage[a * GROUP:(a + 1) * GROUP, :] = fil[:, a * SIDE:(a + 1) * SIDE]
    tr, ti = turn_re, turn_im
    for p in range(GROUP // 2):
        pair = join([stage[pl.ds(2 * p + s, SIDE, stride=GROUP), :] for s in range(2)], 1)
        keep(turned, p, turn_folded(fold_pair(pair, False, fold, fold_hi), tr, ti), 3)
    for p in range(GROUP // 2):
        out = rows_times(turned, p, spread_hi, spread_lo, 3)
        spec[0, 2 * p] = out[:SIDE]
        spec[0, 2 * p + 1] = out[SIDE:]


def load_octets(source, stage):
    for o in range(stage.shape[0]):
        pair = source[:, o // 2 * 2 * OCTET:(o // 2 + 1) * 2 * OCTET, :].astype(F32)
        stage[o] = pair[:, o % 2 * OCTET:(o % 2 + 1) * OCTET].reshape(SIDE * OCTET, SIDE)


def store_octets(result, target):
    for o in range(0, result.shape[0], 2):
        pair = join([result[o + i].reshape(SIDE, OCTET, SIDE) for i in range(2)], 1)
        target[:, o * OCTET:(o + 2) * OCTET, :] = pair.astype(BF16)


def signal_kernel(passes, got, fil, fold, turn_re, turn_im, spread_hi, spread_lo, gather_hi, gather_lo, unfold_hi, unfold_lo,
                  send, cross, skip, stage, result, turned, product, tilted):
    rows = 2 * GROUP
    load_octets(got, stage)
    tr, ti = turn_re, turn_im
    for c in range(GROUP):
        mix = stage[c // OCTET, pl.ds(c % OCTET, SIDE, stride=OCTET), :]
        wgt = stage[(c + GROUP) // OCTET, pl.ds((c + GROUP) % OCTET, SIDE, stride=OCTET), :]
        skip[c:c + 1, :] = jnp.sum(mix * wgt, axis=0, keepdims=True)
        keep(turned, c, turn_folded(fold_pair(join([mix, wgt], 1), True, fold, None), tr, ti), passes[0])
    for c in range(GROUP):
        both = rows_times(turned, c, spread_hi, spread_lo, passes[0])
        mr, mi = both[:SIDE, :SIDE], both[:SIDE, SIDE:]
        wr, wi = both[SIDE:, :SIDE], both[SIDE:, SIDE:]
        fr, fi = fil[0, c, :, :SIDE], fil[0, c, :, SIDE:]
        cross[0, c, :, :SIDE] = wr * mr + wi * mi
        cross[0, c, :, SIDE:] = wi * mr - wr * mi
        keep(product, c, join([
            join([fr * mr - fi * mi, fr * mi + fi * mr], 1),
            join([fr * wr + fi * wi, fr * wi - fi * wr], 1),
        ], 0), passes[1])
    for c in range(GROUP):
        keep(tilted, c, turn_back(rows_times(product, c, gather_hi, gather_lo, passes[1]), tr, ti), passes[2])
    for c in range(GROUP):
        back = times_rows(unfold_hi, unfold_lo, tilted, c, passes[2])
        result[c // OCTET, pl.ds(c % OCTET, SIDE, stride=OCTET), :] = back[:, :SIDE]
        result[(c + GROUP) // OCTET, pl.ds((c + GROUP) % OCTET, SIDE, stride=OCTET), :] = back[:, SIDE:]
    store_octets(result, send)


def grad_kernel(scale, cross, turn_re, turn_im, gather_hi, gather_lo, unfold_hi, unfold_lo, out, stage, product, tilted):
    tr, ti = turn_re, turn_im
    for p in range(GROUP // 2):
        keep(product, p, join([cross[0, 2 * p], cross[0, 2 * p + 1]], 0), 3)
    for p in range(GROUP // 2):
        keep(tilted, p, turn_back(rows_times(product, p, gather_hi, gather_lo, 3), tr, ti), 3)
    for p in range(GROUP // 2):
        back = times_rows(unfold_hi, unfold_lo, tilted, p, 3) * scale
        for s in range(2):
            stage[pl.ds(2 * p + s, SIDE, stride=GROUP), :] = back[:, s * SIDE:(s + 1) * SIDE]
    for a in range(SIDE):
        out[:, a * SIDE:(a + 1) * SIDE] = stage[a * GROUP:(a + 1) * GROUP, :]


def held(signals):
    return pltpu.VMEM((2, signals * SIDE, 2 * SIDE), BF16)


def whole(array):
    return pl.BlockSpec(array.shape, lambda g: (0,) * array.ndim)


FAR = pl.BlockSpec(memory_space=pltpu.HBM)
NEAR = pl.BlockSpec(memory_space=pltpu.VMEM)


def granted(mib):
    return pltpu.CompilerParams(vmem_limit_bytes=mib * 1024 * 1024)


PARAMS = granted(60)


def cost(rows, moved):
    return pl.CostEstimate(flops=2 * rows * 256 * 256, bytes_accessed=moved, transcendentals=0)


def filter_spectra(filters, tab):
    channels, seq = filters.shape
    groups = channels // GROUP
    ops = [tab[k] for k in ("fold", "fold_hi", "turn_re", "turn_im", "spread_hi", "spread_lo")]
    return pl.pallas_call(
        filter_kernel,
        grid=(groups,),
        in_specs=[pl.BlockSpec((GROUP, seq), lambda g: (g, 0))] + [whole(o) for o in ops],
        out_specs=pl.BlockSpec((1, GROUP, SIDE, 2 * SIDE), lambda g: (g, 0, 0, 0)),
        out_shape=jax.ShapeDtypeStruct((groups, GROUP, SIDE, 2 * SIDE), F32),
        scratch_shapes=[pltpu.VMEM((SIDE * GROUP, SIDE), F32), held(GROUP)],
        compiler_params=PARAMS,
        cost_estimate=cost(channels * 5 * SIDE, 6 * channels * seq * 2),
        name="filter_spectra",
    )(filters, *ops)


def convolve(got, spec, tab, passes):
    groups = spec.shape[0]
    channels = groups * GROUP
    ops = [tab[k] for k in ("fold", "turn_re", "turn_im", "spread_hi", "spread_lo", "gather_hi", "gather_lo", "unfold_hi", "unfold_lo")]
    rows = 2 * GROUP
    return pl.pallas_call(
        functools.partial(signal_kernel, passes),
        grid=(groups,),
        in_specs=[pl.BlockSpec((SIDE, rows, SIDE), lambda g: (0, g, 0)),
                  pl.BlockSpec((1, GROUP, SIDE, 2 * SIDE), lambda g: (g, 0, 0, 0))] + [whole(o) for o in ops],
        out_specs=[pl.BlockSpec((SIDE, rows, SIDE), lambda g: (0, g, 0)),
                   pl.BlockSpec((1, GROUP, SIDE, 2 * SIDE), lambda g: (g, 0, 0, 0)),
                   pl.BlockSpec((GROUP, SIDE), lambda g: (g, 0))],
        out_shape=[pltpu.HBM((SIDE, 2 * channels, SIDE), BF16),
                   pltpu.HBM(spec.shape, F32),
                   jax.ShapeDtypeStruct((channels, SIDE), F32)],
        scratch_shapes=[pltpu.VMEM((rows // OCTET, SIDE * OCTET, SIDE), F32)] * 2 + [held(2 * GROUP)] * 3,
        compiler_params=granted(48),
        cost_estimate=cost(channels * 17 * SIDE, 12 * channels * SIDE * SIDE),
        name="convolve",
    )(got, spec, *ops)


def filter_gradient(cross, tab, scale):
    groups = cross.shape[0]
    channels = groups * GROUP
    ops = [tab[k] for k in ("turn_re", "turn_im", "gather_hi", "gather_lo", "unfold_hi", "unfold_lo")]
    return pl.pallas_call(
        functools.partial(grad_kernel, scale),
        grid=(groups,),
        in_specs=[pl.BlockSpec((1, GROUP, SIDE, 2 * SIDE), lambda g: (g, 0, 0, 0))] + [whole(o) for o in ops],
        out_specs=pl.BlockSpec((GROUP, SIDE * SIDE), lambda g: (g, 0)),
        out_shape=jax.ShapeDtypeStruct((channels, SIDE * SIDE), F32),
        scratch_shapes=[pltpu.VMEM((SIDE * GROUP, SIDE), F32), held(GROUP), held(GROUP)],
        compiler_params=PARAMS,
        cost_estimate=cost(channels * 5 * SIDE, 12 * channels * SIDE * SIDE),
        name="filter_gradient",
    )(cross, *ops)


PIECES = 8


def chunk(array, i):
    size = array.shape[0] // PIECES
    return array.at[pl.ds(i * size, size)]


def fetches(sources, stores, sems):
    return [[pltpu.make_async_copy(chunk(s, i), chunk(d, i), sems.at[j, i]) for j, (s, d) in enumerate(zip(sources, stores))]
            for i in range(PIECES)]


def products_kernel(query, key_in, value_in, cotangent, out, q, k, v, c, both, in_sem, out_sem):
    loads = fetches((query, key_in, value_in, cotangent), (q, k, v, c), in_sem)
    stores = [s[0] for s in fetches((both,), (out,), out_sem)]
    for group in loads:
        for copy in group:
            copy.start()
    for i in range(PIECES):
        for copy in loads[i]:
            copy.wait()
        qi, ki, vi, ci = [chunk(x, i)[...].astype(F32) for x in (q, k, v, c)]
        pair = jnp.stack([x.reshape(-1, GROUP, SIDE) for x in (ki * vi, ci * qi)], axis=1)
        chunk(both, i)[...] = pair.reshape(chunk(both, i).shape).astype(BF16)
        stores[i].start()
    for copy in stores:
        copy.wait()


def products(query, key_in, value_in, cotangent, own):
    channels = query.shape[0]
    sent = (channels // own, 2 * own, SIDE)
    return pl.pallas_call(
        products_kernel,
        in_specs=[FAR] * 4,
        out_specs=FAR,
        out_shape=jax.ShapeDtypeStruct(sent, BF16),
        scratch_shapes=[pltpu.VMEM(query.shape, BF16)] * 4 + [pltpu.VMEM(sent, BF16)]
        + [pltpu.SemaphoreType.DMA((4, PIECES)), pltpu.SemaphoreType.DMA((1, PIECES))],
        compiler_params=PARAMS,
        cost_estimate=pl.CostEstimate(flops=2 * channels * SIDE, bytes_accessed=12 * channels * SIDE, transcendentals=0),
        name="products",
    )(query, key_in, value_in, cotangent)


def finish_kernel(query, key_in, value_in, cotangent, got, gain, output, grad_query, grad_key, grad_value,
                  q, k, v, c, spread, out_a, out_b, out_c, out_d, in_sem, out_sem):
    results = (out_a, out_b, out_c, out_d)
    loads = fetches((query, key_in, value_in, cotangent), (q, k, v, c), in_sem)
    stores = fetches(results, (output, grad_query, grad_key, grad_value), out_sem)
    for group in loads:
        for copy in group:
            copy.start()
    for i in range(gain.shape[0]):
        spread[i * SIDE:(i + 1) * SIDE, :] = jnp.broadcast_to(gain[i:i + 1, :], (SIDE, SIDE)).T
    for i in range(PIECES):
        for copy in loads[i]:
            copy.wait()
        qi, ki, vi, ci, pair = [chunk(x, i)[...].astype(F32) for x in (q, k, v, c, got)]
        pair = pair.reshape(-1, 2, GROUP, SIDE)
        conv, back = pair[:, 0].reshape(qi.shape), pair[:, 1].reshape(qi.shape)
        g = chunk(spread, i)[...]
        inner = conv + g * (ki * vi).astype(BF16).astype(F32)
        dmixed = back + g * (ci * qi).astype(BF16).astype(F32)
        for store, value in zip(results, (qi * inner, ci * inner, dmixed * vi, dmixed * ki)):
            chunk(store, i)[...] = value.astype(BF16)
        for copy in stores[i]:
            copy.start()
    for group in stores:
        for copy in group:
            copy.wait()


def finish(query, key_in, value_in, cotangent, got, gain):
    channels = query.shape[0]
    return pl.pallas_call(
        finish_kernel,
        in_specs=[FAR] * 4 + [NEAR] * 2,
        out_specs=[FAR] * 4,
        out_shape=[jax.ShapeDtypeStruct(query.shape, BF16)] * 4,
        scratch_shapes=[pltpu.VMEM(query.shape, BF16)] * 4 + [pltpu.VMEM(query.shape, F32)]
        + [pltpu.VMEM(query.shape, BF16)] * 4
        + [pltpu.SemaphoreType.DMA((4, PIECES)), pltpu.SemaphoreType.DMA((4, PIECES))],
        compiler_params=granted(61),
        cost_estimate=pl.CostEstimate(flops=10 * channels * SIDE, bytes_accessed=20 * channels * SIDE, transcendentals=0),
        name="finish",
    )(query, key_in, value_in, cotangent, got, gain)


def exchange(blocks):
    return lax.all_to_all(blocks, ("node", "local"), split_axis=0, concat_axis=0, tiled=True)


def local(query, key_in, value_in, filters, skip_gain, cotangent):
    tab = tables()
    scale = float(filters.shape[1]) ** -0.5
    got = exchange(products(query, key_in, value_in, cotangent, filters.shape[0]))
    spec = filter_spectra(filters, tab)
    gain = skip_gain.reshape(-1, SIDE)
    send, cross, skip = convolve(got, spec, tab, (3, 3, 3))
    back = exchange(send)
    grad_filters = filter_gradient(cross, tab, scale)
    grad_skip = jnp.sum(skip.reshape(-1, SIDE), axis=1) * scale
    return (*finish(query, key_in, value_in, cotangent, back, gain), grad_filters, grad_skip)


def solution(mesh):
    tokens = P(None, ("node", "local"))
    return jax.shard_map(
        local,
        mesh=mesh,
        in_specs=(tokens, tokens, tokens, P(("node", "local"), None), P(), tokens),
        out_specs=(tokens, tokens, tokens, tokens, P(("node", "local"), None), P(("node", "local"))),
        check_vma=False,
    )
```

time: 114 us -> 101 us (0.89)
  other arithmetic: 9.36 us -> 0.63 us
  local copies, waits for them, and re-layouts: 6.06 us -> 0.06 us
  waiting for transfers between devices: 40 us -> 45.6 us
  Pallas kernels: 41.1 us -> 37 us
    pallas_call x1, Pallas kernels: 25.7 us -> 14.7 us  [convolve(): pl.pallas_call(functools.partial(signal_kernel, passes), grid=(groups,),...]
    pallas_call x0 -> x2, Pallas kernels: none -> 9.2 us  [the longest x1 5.62 us: finish(): pl.pallas_call(finish_kernel, in_specs=[FAR] * 4 + [NEAR] * 2, out_specs=...]
    convert_element_type x2 -> x0, other arithmetic: 6.83 us -> none  [the longest x1 4.11 us: local(): grad_value = (dmixed * key_in.astype(F32)).astype(BF16)]
    all_to_all x2, waiting for transfers between devices: 40 us -> 45.6 us  [exchange(): lax.all_to_all(blocks, ('node', 'local'), split_axis=0, concat_axis=0, ti...]
    unnamed x38 -> x18, local copies, waits for them, and re-layouts: 5.69 us -> 0.06 us
    pallas_call x1, Pallas kernels: 8.66 us -> 6.39 us  [filter_gradient(): pl.pallas_call(functools.partial(grad_kernel, scale), grid=(groups,), in_...]
    another operation x1 -> x0, other arithmetic: 1.9 us -> none  [interleave(): return jnp.stack(parts, axis=2).reshape(SIDE, -1, SIDE)]
  transfers between devices with their start and end apart: 2 -> 2, of which waited for: 2 -> 2; matrix products, arithmetic and copies ran while one was open for 1% -> 1% of each run, Pallas kernels for 14% -> 13%
where the time goes in v1:
time: 101 us
  waiting for transfers between devices  45.6 us (45%)
  Pallas kernels  37 us (37%)
  starting transfers between devices  16.9 us (17%)
    all_to_all x2, waiting for transfers between devices, exchange(): lax.all_to_all(blocks, ('node', 'local'), split_axis=0, concat_axis=0, ti...  45.6 us
    all_to_all x2, starting transfers between devices, exchange(): lax.all_to_all(blocks, ('node', 'local'), split_axis=0, concat_axis=0, ti...  16.9 us
    pallas_call x1, Pallas kernels, convolve(): pl.pallas_call(functools.partial(signal_kernel, passes), grid=(groups,),...  14.7 us
    pallas_call x1, Pallas kernels, filter_spectra(): pl.pallas_call(filter_kernel, grid=(groups,), in_specs=[pl.BlockSpec((GRO...  6.68 us
    pallas_call x1, Pallas kernels, filter_gradient(): pl.pallas_call(functools.partial(grad_kernel, scale), grid=(groups,), in_...  6.39 us
    pallas_call x1, Pallas kernels, finish(): pl.pallas_call(finish_kernel, in_specs=[FAR] * 4 + [NEAR] * 2, out_specs=...  5.62 us
    pallas_call x1, Pallas kernels, products(): pl.pallas_call(products_kernel, in_specs=[FAR] * 4, out_specs=FAR, out_sh...  3.58 us
  transfers between devices with their start and end apart: 2, of which 2 were waited for; matrix products, arithmetic and copies ran while one was open for 1% of the time, Pallas kernels for 13%

profile of v1, /device:TPU:0, one launch (start us, length us, event | category | flops | bytes accessed | tf_op | source)
XLA Modules:
  0.0 101.0 jit_solution(13475059338563091532)
XLA Ops:
  0.6 3.6 %products.1 = bf16[128,64,128]{2,1,0:T(8,128)(2,1)} custom-call(bf16[4096,128]{1,0:T(8,128)(2,1)} %query.3, bf16[4096,128]{1,0:T(8,128)(2,1)} %key_in.3, bf16[4096,128]{1,0:T(8,128)(2,1)} %value_in.3, bf16[4096,128]{1,0:T(8,128)(2,1)} %cotangent.3), custom_call_target="tpu_custom_call" | custom-call | flops 1048576 | bytes 6291456 | tf_op jit(solution)/shard_map/products/pallas_call | solution.py:292
  4.2 11.1 %all-to-all-start = ((bf16[128,64,128]{2,1,0:T(8,128)(2,1)}), bf16[128,64,128]{2,1,0:T(8,128)(2,1)S(1)}, u32[]{:S(2)}, u32[]{:S(2)}) async-start(bf16[128,64,128]{2,1,0:T(8,128)(2,1)} %products.1), calls=%async_computation | async-start | bytes 4194304 | tf_op jit(solution)/shard_map/all_to_all | solution.py:350
  15.4 0.0 copy-start
  15.4 0.0 copy-start.1
  15.4 0.0 copy-start.2
  15.4 0.0 copy-start.3
  15.4 0.0 copy-start.4
  15.4 0.0 copy-start.5
  15.5 0.0 copy-start.6
  15.5 0.0 copy-start.7
  15.5 0.0 copy-start.8
  15.5 6.7 %filter_spectra.1.fil = f32[4,8,128,256]{3,2,1,0:T(8,128)} custom-call(f32[32,16384]{1,0:T(8,128)} %fil.1, bf16[256,256]{1,0:T(8,128)(2,1)} %constant.24.clone.fold, bf16[256,128]{1,0:T(8,128)(2,1)} %constant.25.clone.fold_hi, f32[128,128]{1,0:T(8,128)} %constant.26.clone.turn_re, f32[128,128]{1,0:T(8,128)} %constant.27.clone.turn_im, ...), custom_call_target="tpu_custom_call" | custom-call | flops 2684354560 | bytes 6291456 | tf_op jit(solution)/shard_map/filter_spectra/pallas_call | solution.py:206
  22.2 23.1 %all-to-all-done.got = bf16[128,64,128]{2,1,0:T(8,128)(2,1)S(1)} async-done(((bf16[128,64,128]{2,1,0:T(8,128)(2,1)}), bf16[128,64,128]{2,1,0:T(8,128)(2,1)S(1)}, u32[]{:S(2)}, u32[]{:S(2)}) %all-to-all-start) | async-done | bytes 2097184 | tf_op jit(solution)/shard_map/all_to_all | solution.py:350
  45.3 0.0 copy-done
  45.3 0.0 copy-done.1
  45.3 0.0 copy-done.2
  45.3 0.0 copy-done.3
  45.3 0.0 copy-done.4
  45.3 0.0 copy-done.5
  45.3 0.0 copy-done.6
  45.4 0.0 copy-done.7
  45.4 0.0 copy-done.8
  45.4 14.7 %convolve.1 = (bf16[128,64,128]{2,1,0:T(8,128)(2,1)}, f32[4,8,128,256]{3,2,1,0:T(8,128)}, f32[32,128]{1,0:T(8,128)S(1)}) custom-call(bf16[128,64,128]{2,1,0:T(8,128)(2,1)S(1)} %all-to-all-done.got, f32[4,8,128,256]{3,2,1,0:T(8,128)} %filter_spectra.1.fil, bf16[256,256]{1,0:T(8,128)(2,1)S(1)} %copy-done.4, f32[128,128]{1,0:T(8,128)S(1)} %copy-done.6, ...), custom_call_target="tpu_custom_call" | custom-call | flops 9126805504 | bytes 6291456 | tf_op jit(solution)/shard_map/convolve/pallas_call | solution.py:224
  60.1 5.8 %all-to-all-start.1 = ((bf16[128,64,128]{2,1,0:T(8,128)(2,1)}), bf16[128,64,128]{2,1,0:T(8,128)(2,1)}, u32[]{:S(2)}, u32[]{:S(2)}) async-start(bf16[128,64,128]{2,1,0:T(8,128)(2,1)} %get-tuple-element.13), calls=%async_computation.1 | async-start | bytes 4194304 | tf_op jit(solution)/shard_map/all_to_all | solution.py:350
  65.9 0.1 reduce_sum.9
  66.0 0.5 broadcast_multiply_fusion
  66.5 6.4 %filter_gradient.1 = f32[32,16384]{1,0:T(8,128)} custom-call(f32[4,8,128,256]{3,2,1,0:T(8,128)} %get-tuple-element.18.cross, f32[128,128]{1,0:T(8,128)} %constant.26.clone.turn_re, f32[128,128]{1,0:T(8,128)} %constant.27.clone.turn_im, bf16[256,256]{1,0:T(8,128)(2,1)} %constant.30.clone.gather_hi, bf16[256,256]{1,0:T(8,128)(2,1)} %constant.31.clone.gather_lo, ...), custom_call_target="tpu_custom_call" | custom-call | flops 2684354560 | bytes 6291456 | tf_op jit(solution)/shard_map/filter_gradient/pallas_call | solution.py:246
  72.9 22.5 %all-to-all-done.1.got = bf16[128,64,128]{2,1,0:T(8,128)(2,1)} async-done(((bf16[128,64,128]{2,1,0:T(8,128)(2,1)}), bf16[128,64,128]{2,1,0:T(8,128)(2,1)}, u32[]{:S(2)}, u32[]{:S(2)}) %all-to-all-start.1) | async-done | bytes 2097184 | tf_op jit(solution)/shard_map/all_to_all | solution.py:350
  95.4 5.6 %finish.1 = (bf16[4096,128]{1,0:T(8,128)(2,1)}, bf16[4096,128]{1,0:T(8,128)(2,1)}, bf16[4096,128]{1,0:T(8,128)(2,1)}, bf16[4096,128]{1,0:T(8,128)(2,1)}) custom-call(bf16[4096,128]{1,0:T(8,128)(2,1)} %query.3, bf16[4096,128]{1,0:T(8,128)(2,1)} %key_in.3, bf16[4096,128]{1,0:T(8,128)(2,1)} %value_in.3, bf16[4096,128]{1,0:T(8,128)(2,1)} %cotangent.3, ...), custom_call_target="tpu_custom_call" | custom-call | flops 5242880 | bytes 10485760 | tf_op jit(solution)/shard_map/finish/pallas_call | solution.py:335
Async XLA Ops:
  4.2 41.1 %all-to-all-start = ((bf16[128,64,128]{2,1,0:T(8,128)(2,1)}), bf16[128,64,128]{2,1,0:T(8,128)(2,1)S(1)}, u32[]{:S(2)}, u32[]{:S(2)}) async-start(bf16[128,64,128]{2,1,0:T(8,128)(2,1)} %products.1), calls=%async_computation | async-start | bytes 4194304 | tf_op jit(solution)/shard_map/all_to_all | solution.py:350
  15.4 29.9 %copy-start = (bf16[256,256]{1,0:T(8,128)(2,1)S(1)}, bf16[256,256]{1,0:T(8,128)(2,1)}, u32[]{:S(2)}) copy-start(bf16[256,256]{1,0:T(8,128)(2,1)} %constant.31.clone.gather_lo) | copy-start | bytes 393220
  15.4 29.9 %copy-start.1 = (bf16[256,256]{1,0:T(8,128)(2,1)S(1)}, bf16[256,256]{1,0:T(8,128)(2,1)}, u32[]{:S(2)}) copy-start(bf16[256,256]{1,0:T(8,128)(2,1)} %constant.30.clone.gather_hi) | copy-start | bytes 393220
  15.4 29.9 %copy-start.2 = (bf16[256,256]{1,0:T(8,128)(2,1)S(1)}, bf16[256,256]{1,0:T(8,128)(2,1)}, u32[]{:S(2)}) copy-start(bf16[256,256]{1,0:T(8,128)(2,1)} %constant.29.clone.spread_lo) | copy-start | bytes 393220
  15.4 29.9 %copy-start.3 = (bf16[256,256]{1,0:T(8,128)(2,1)S(1)}, bf16[256,256]{1,0:T(8,128)(2,1)}, u32[]{:S(2)}) copy-start(bf16[256,256]{1,0:T(8,128)(2,1)} %constant.28.clone.spread_hi) | copy-start | bytes 393220
  15.4 29.9 %copy-start.4 = (bf16[256,256]{1,0:T(8,128)(2,1)S(1)}, bf16[256,256]{1,0:T(8,128)(2,1)}, u32[]{:S(2)}) copy-start(bf16[256,256]{1,0:T(8,128)(2,1)} %constant.24.clone.fold) | copy-start | bytes 393220
  15.4 29.9 %copy-start.5 = (f32[128,128]{1,0:T(8,128)S(1)}, f32[128,128]{1,0:T(8,128)}, u32[]{:S(2)}) copy-start(f32[128,128]{1,0:T(8,128)} %constant.27.clone.turn_im) | copy-start | bytes 196612
  15.5 29.9 %copy-start.6 = (f32[128,128]{1,0:T(8,128)S(1)}, f32[128,128]{1,0:T(8,128)}, u32[]{:S(2)}) copy-start(f32[128,128]{1,0:T(8,128)} %constant.26.clone.turn_re) | copy-start | bytes 196612
  15.5 29.9 %copy-start.7 = (bf16[128,256]{1,0:T(8,128)(2,1)S(1)}, bf16[128,256]{1,0:T(8,128)(2,1)}, u32[]{:S(2)}) copy-start(bf16[128,256]{1,0:T(8,128)(2,1)} %constant.33.clone.unfold_lo) | copy-start | bytes 196612
  15.5 29.9 %copy-start.8 = (bf16[128,256]{1,0:T(8,128)(2,1)S(1)}, bf16[128,256]{1,0:T(8,128)(2,1)}, u32[]{:S(2)}) copy-start(bf16[128,256]{1,0:T(8,128)(2,1)} %constant.32.clone.unfold_hi) | copy-start | bytes 196612
  60.1 35.3 %all-to-all-start.1 = ((bf16[128,64,128]{2,1,0:T(8,128)(2,1)}), bf16[128,64,128]{2,1,0:T(8,128)(2,1)}, u32[]{:S(2)}, u32[]{:S(2)}) async-start(bf16[128,64,128]{2,1,0:T(8,128)(2,1)} %get-tuple-element.13), calls=%async_computation.1 | async-start | bytes 4194304 | tf_op jit(solution)/shard_map/all_to_all | solution.py:350

commit v2 on v1

--- a/solution.py
+++ b/solution.py
@@ -88,23 +88,23 @@
 def rows_times(store, c, hi, lo, passes):
     rows = pl.ds(c * 2 * SIDE, 2 * SIDE)
     high = store[0, rows, :]
-    total = dot(high, hi[...])
+    lhs, rhs = [high], [hi[...]]
     if passes >= 2:
-        total = total + dot(high, lo[...])
+        lhs, rhs = lhs + [high], rhs + [lo[...]]
     if passes >= 3:
-        total = total + dot(store[1, rows, :], hi[...])
-    return total
+        lhs, rhs = lhs + [store[1, rows, :]], rhs + [hi[...]]
+    return dot(join(lhs, 1), join(rhs, 0))
 
 
 def times_rows(hi, lo, store, c, passes):
     rows = pl.ds(c * 2 * SIDE, 2 * SIDE)
     high = store[0, rows, :]
-    total = dot(hi[...], high)
+    lhs, rhs = [hi[...]], [high]
     if passes >= 2:
-        total = total + dot(lo[...], high)
+        lhs, rhs = lhs + [lo[...]], rhs + [high]
     if passes >= 3:
-        total = total + dot(hi[...], store[1, rows, :])
-    return total
+        lhs, rhs = lhs + [hi[...]], rhs + [store[1, rows, :]]
+    return dot(join(lhs, 1), join(rhs, 0))
 
 
 def filter_kernel(fil, fold, fold_hi, turn_re, turn_im, spread_hi, spread_lo, spec, stage, turned):
@@ -147,8 +147,8 @@
         mr, mi = both[:SIDE, :SIDE], both[:SIDE, SIDE:]
         wr, wi = both[SIDE:, :SIDE], both[SIDE:, SIDE:]
         fr, fi = fil[0, c, :, :SIDE], fil[0, c, :, SIDE:]
-        cross[0, c, :, :SIDE] = wr * mr + wi * mi
-        cross[0, c, :, SIDE:] = wi * mr - wr * mi
+        cross[0, c, :, :SIDE] = (wr * mr + wi * mi).astype(BF16)
+        cross[0, c, :, SIDE:] = (wi * mr - wr * mi).astype(BF16)
         keep(product, c, join([
             join([fr * mr - fi * mi, fr * mi + fi * mr], 1),
             join([fr * wr + fi * wi, fr * wi - fi * wr], 1),
@@ -162,12 +162,11 @@
     store_octets(result, send)
 
 
-def grad_kernel(scale, cross, turn_re, turn_im, gather_hi, gather_lo, unfold_hi, unfold_lo, out, stage, product, tilted):
+def grad_kernel(scale, cross, turn_re, turn_im, gather_hi, gather_lo, unfold_hi, unfold_lo, out, stage, tilted):
     tr, ti = turn_re, turn_im
+    pairs = cross.reshape(1, GROUP * SIDE, 2 * SIDE)
     for p in range(GROUP // 2):
-        keep(product, p, join([cross[0, 2 * p], cross[0, 2 * p + 1]], 0), 3)
-    for p in range(GROUP // 2):
-        keep(tilted, p, turn_back(rows_times(product, p, gather_hi, gather_lo, 3), tr, ti), 3)
+        keep(tilted, p, turn_back(rows_times(pairs, p, gather_hi, gather_lo, 2), tr, ti), 3)
     for p in range(GROUP // 2):
         back = times_rows(unfold_hi, unfold_lo, tilted, p, 3) * scale
         for s in range(2):
@@ -230,7 +229,7 @@
                    pl.BlockSpec((1, GROUP, SIDE, 2 * SIDE), lambda g: (g, 0, 0, 0)),
                    pl.BlockSpec((GROUP, SIDE), lambda g: (g, 0))],
         out_shape=[pltpu.HBM((SIDE, 2 * channels, SIDE), BF16),
-                   pltpu.HBM(spec.shape, F32),
+                   pltpu.HBM(spec.shape, BF16),
                    jax.ShapeDtypeStruct((channels, SIDE), F32)],
         scratch_shapes=[pltpu.VMEM((rows // OCTET, SIDE * OCTET, SIDE), F32)] * 2 + [held(2 * GROUP)] * 3,
         compiler_params=granted(48),
@@ -249,14 +248,14 @@
         in_specs=[pl.BlockSpec((1, GROUP, SIDE, 2 * SIDE), lambda g: (g, 0, 0, 0))] + [whole(o) for o in ops],
         out_specs=pl.BlockSpec((GROUP, SIDE * SIDE), lambda g: (g, 0)),
         out_shape=jax.ShapeDtypeStruct((channels, SIDE * SIDE), F32),
-        scratch_shapes=[pltpu.VMEM((SIDE * GROUP, SIDE), F32), held(GROUP), held(GROUP)],
+        scratch_shapes=[pltpu.VMEM((SIDE * GROUP, SIDE), F32), held(GROUP)],
         compiler_params=PARAMS,
         cost_estimate=cost(channels * 5 * SIDE, 12 * channels * SIDE * SIDE),
         name="filter_gradient",
     )(cross, *ops)
 
 
-PIECES = 8
+PIECES = 4
 
 
 def chunk(array, i):
@@ -303,9 +302,9 @@
 
 
 def finish_kernel(query, key_in, value_in, cotangent, got, gain, output, grad_query, grad_key, grad_value,
-                  q, k, v, c, spread, out_a, out_b, out_c, out_d, in_sem, out_sem):
+                  c, both, spread, out_a, out_b, out_c, out_d, in_sem, out_sem):
     results = (out_a, out_b, out_c, out_d)
-    loads = fetches((query, key_in, value_in, cotangent), (q, k, v, c), in_sem)
+    loads = fetches((cotangent, got), (c, both), in_sem)
     stores = fetches(results, (output, grad_query, grad_key, grad_value), out_sem)
     for group in loads:
         for copy in group:
@@ -315,7 +314,7 @@
     for i in range(PIECES):
         for copy in loads[i]:
             copy.wait()
-        qi, ki, vi, ci, pair = [chunk(x, i)[...].astype(F32) for x in (q, k, v, c, got)]
+        qi, ki, vi, ci, pair = [chunk(x, i)[...].astype(F32) for x in (query, key_in, value_in, c, both)]
         pair = pair.reshape(-1, 2, GROUP, SIDE)
         conv, back = pair[:, 0].reshape(qi.shape), pair[:, 1].reshape(qi.shape)
         g = chunk(spread, i)[...]
@@ -334,13 +333,13 @@
     channels = query.shape[0]
     return pl.pallas_call(
         finish_kernel,
-        in_specs=[FAR] * 4 + [NEAR] * 2,
+        in_specs=[NEAR] * 3 + [FAR] * 2 + [NEAR],
         out_specs=[FAR] * 4,
         out_shape=[jax.ShapeDtypeStruct(query.shape, BF16)] * 4,
-        scratch_shapes=[pltpu.VMEM(query.shape, BF16)] * 4 + [pltpu.VMEM(query.shape, F32)]
+        scratch_shapes=[pltpu.VMEM(query.shape, BF16), pltpu.VMEM(got.shape, BF16), pltpu.VMEM(query.shape, F32)]
         + [pltpu.VMEM(query.shape, BF16)] * 4
-        + [pltpu.SemaphoreType.DMA((4, PIECES)), pltpu.SemaphoreType.DMA((4, PIECES))],
-        compiler_params=granted(61),
+        + [pltpu.SemaphoreType.DMA((2, PIECES)), pltpu.SemaphoreType.DMA((4, PIECES))],
+        compiler_params=granted(48),
         cost_estimate=pl.CostEstimate(flops=10 * channels * SIDE, bytes_accessed=20 * channels * SIDE, transcendentals=0),
         name="finish",
     )(query, key_in, value_in, cotangent, got, gain)
@@ -356,7 +355,7 @@
     got = exchange(products(query, key_in, value_in, cotangent, filters.shape[0]))
     spec = filter_spectra(filters, tab)
     gain = skip_gain.reshape(-1, SIDE)
-    send, cross, skip = convolve(got, spec, tab, (3, 3, 3))
+    send, cross, skip = convolve(got, spec, tab, (2, 2, 2))
     back = exchange(send)
     grad_filters = filter_gradient(cross, tab, scale)
     grad_skip = jnp.sum(skip.reshape(-1, SIDE), axis=1) * scale

time: 101 us -> 96.9 us (0.959)
  Pallas kernels: 37 us -> 30.5 us
  local copies, waits for them, and re-layouts: 0.06 us -> 1.3 us
    pallas_call x1, Pallas kernels: 14.7 us -> 11.1 us  [convolve(): pl.pallas_call(functools.partial(signal_kernel, passes), grid=(groups,),...]
    pallas_call x1, Pallas kernels: 5.62 us -> 3.72 us  [finish(): pl.pallas_call(finish_kernel, in_specs=[NEAR] * 3 + [FAR] * 2 + [NEAR], o...]
    unnamed x18 -> x28, local copies, waits for them, and re-layouts: 0.06 us -> 1.3 us
where the time goes in v2:
time: 96.9 us; the launch traced here: 96.4 us
  waiting for transfers between devices  46.2 us (48%)
  Pallas kernels  30.5 us (31%)
  starting transfers between devices  16.9 us (17%)
  local copies, waits for them, and re-layouts  1.3 us (1%)
    all_to_all x2, waiting for transfers between devices, exchange(): lax.all_to_all(blocks, ('node', 'local'), split_axis=0, concat_axis=0, ti...  46.2 us
    all_to_all x2, starting transfers between devices, exchange(): lax.all_to_all(blocks, ('node', 'local'), split_axis=0, concat_axis=0, ti...  16.9 us
    pallas_call x1, Pallas kernels, convolve(): pl.pallas_call(functools.partial(signal_kernel, passes), grid=(groups,),...  11.1 us
    pallas_call x1, Pallas kernels, filter_spectra(): pl.pallas_call(filter_kernel, grid=(groups,), in_specs=[pl.BlockSpec((GRO...  6.67 us
    pallas_call x1, Pallas kernels, filter_gradient(): pl.pallas_call(functools.partial(grad_kernel, scale), grid=(groups,), in_...  5.75 us
    pallas_call x1, Pallas kernels, finish(): pl.pallas_call(finish_kernel, in_specs=[NEAR] * 3 + [FAR] * 2 + [NEAR], o...  3.72 us
    pallas_call x1, Pallas kernels, products(): pl.pallas_call(products_kernel, in_specs=[FAR] * 4, out_specs=FAR, out_sh...  3.23 us
  transfers between devices with their start and end apart: 2, of which 2 were waited for; matrix products, arithmetic and copies ran while one was open for 1% of the time, Pallas kernels for 13%

profile of v2, /device:TPU:0, one launch (start us, length us, event | category | flops | bytes accessed | tf_op | source)
XLA Modules:
  0.0 96.4 jit_solution(14501432564270421058)
XLA Ops:
  0.6 3.2 %products.1 = bf16[128,64,128]{2,1,0:T(8,128)(2,1)} custom-call(bf16[4096,128]{1,0:T(8,128)(2,1)} %query.3, bf16[4096,128]{1,0:T(8,128)(2,1)} %key_in.3, bf16[4096,128]{1,0:T(8,128)(2,1)} %value_in.3, bf16[4096,128]{1,0:T(8,128)(2,1)} %cotangent.3), custom_call_target="tpu_custom_call" | custom-call | flops 1048576 | bytes 6291456 | tf_op jit(solution)/shard_map/products/pallas_call | solution.py:291
  3.9 11.1 %all-to-all-start = ((bf16[128,64,128]{2,1,0:T(8,128)(2,1)}), bf16[128,64,128]{2,1,0:T(8,128)(2,1)S(1)}, u32[]{:S(2)}, u32[]{:S(2)}) async-start(bf16[128,64,128]{2,1,0:T(8,128)(2,1)} %products.1), calls=%async_computation | async-start | bytes 4194304 | tf_op jit(solution)/shard_map/all_to_all | solution.py:349
  15.0 0.0 copy-start.5
  15.0 0.0 copy-start.6
  15.0 0.0 copy-start.7
  15.1 0.0 copy-start.8
  15.1 0.0 copy-start.9
  15.1 0.0 copy-start.10
  15.1 0.0 copy-start.11
  15.1 0.0 copy-start.12
  15.1 0.0 copy-start.13
  15.1 6.7 %filter_spectra.1.fil = f32[4,8,128,256]{3,2,1,0:T(8,128)} custom-call(f32[32,16384]{1,0:T(8,128)} %fil.1, bf16[256,256]{1,0:T(8,128)(2,1)} %constant.24.clone.fold, bf16[256,128]{1,0:T(8,128)(2,1)} %constant.25.clone.fold_hi, f32[128,128]{1,0:T(8,128)} %constant.26.clone.turn_re, f32[128,128]{1,0:T(8,128)} %constant.27.clone.turn_im, ...), custom_call_target="tpu_custom_call" | custom-call | flops 2684354560 | bytes 6291456 | tf_op jit(solution)/shard_map/filter_spectra/pallas_call | solution.py:205
  21.8 23.1 %all-to-all-done.got = bf16[128,64,128]{2,1,0:T(8,128)(2,1)S(1)} async-done(((bf16[128,64,128]{2,1,0:T(8,128)(2,1)}), bf16[128,64,128]{2,1,0:T(8,128)(2,1)S(1)}, u32[]{:S(2)}, u32[]{:S(2)}) %all-to-all-start) | async-done | bytes 2097184 | tf_op jit(solution)/shard_map/all_to_all | solution.py:349
  45.0 0.0 copy-done.5
  45.0 0.0 copy-done.6
  45.0 0.0 copy-done.7
  45.0 0.0 copy-done.8
  45.0 0.0 copy-done.9
  45.0 0.0 copy-done.10
  45.0 0.0 copy-done.11
  45.0 0.0 copy-done.12
  45.0 0.0 copy-done.13
  45.0 11.1 %convolve.1 = (bf16[128,64,128]{2,1,0:T(8,128)(2,1)}, bf16[4,8,128,256]{3,2,1,0:T(8,128)(2,1)}, f32[32,128]{1,0:T(8,128)S(1)}) custom-call(bf16[128,64,128]{2,1,0:T(8,128)(2,1)S(1)} %all-to-all-done.got, f32[4,8,128,256]{3,2,1,0:T(8,128)} %filter_spectra.1.fil, bf16[256,256]{1,0:T(8,128)(2,1)S(1)} %copy-done.9, f32[128,128]{1,0:T(8,128)S(1)} %copy-done.11, ...), custom_call_target="tpu_custom_call" | custom-call | flops 9126805504 | bytes 6291456 | tf_op jit(solution)/shard_map/convolve/pallas_call | solution.py:223
  56.1 5.8 %all-to-all-start.1 = ((bf16[128,64,128]{2,1,0:T(8,128)(2,1)}), bf16[128,64,128]{2,1,0:T(8,128)(2,1)}, u32[]{:S(2)}, u32[]{:S(2)}) async-start(bf16[128,64,128]{2,1,0:T(8,128)(2,1)} %get-tuple-element.13), calls=%async_computation.1 | async-start | bytes 4194304 | tf_op jit(solution)/shard_map/all_to_all | solution.py:349
  61.9 0.1 reduce_sum.9
  62.0 0.5 broadcast_multiply_fusion
  62.6 5.8 %filter_gradient.1 = f32[32,16384]{1,0:T(8,128)} custom-call(bf16[4,8,128,256]{3,2,1,0:T(8,128)(2,1)} %get-tuple-element.18.cross, f32[128,128]{1,0:T(8,128)} %constant.26.clone.turn_re, f32[128,128]{1,0:T(8,128)} %constant.27.clone.turn_im, bf16[256,256]{1,0:T(8,128)(2,1)} %constant.30.clone.gather_hi, bf16[256,256]{1,0:T(8,128)(2,1)} %constant.31.clone.gather_lo, ...), custom_call_target="tpu_custom_call" | custom-call | flops 2684354560 | bytes 6291456 | tf_op jit(solution)/shard_map/filter_gradient/pallas_call | solution.py:245
  68.3 23.1 %all-to-all-done.1.got = bf16[128,64,128]{2,1,0:T(8,128)(2,1)} async-done(((bf16[128,64,128]{2,1,0:T(8,128)(2,1)}), bf16[128,64,128]{2,1,0:T(8,128)(2,1)}, u32[]{:S(2)}, u32[]{:S(2)}) %all-to-all-start.1) | async-done | bytes 2097184 | tf_op jit(solution)/shard_map/all_to_all | solution.py:349
  91.4 0.0 copy-done
  91.4 0.0 copy-start.3
  91.4 1.2 %copy-done.3 = bf16[4096,128]{1,0:T(8,128)(2,1)S(1)} copy-done((bf16[4096,128]{1,0:T(8,128)(2,1)S(1)}, bf16[4096,128]{1,0:T(8,128)(2,1)}, u32[]{:S(2)}) %copy-start.3) | copy-done | bytes 1048600
  92.7 3.7 %finish.1 = (bf16[4096,128]{1,0:T(8,128)(2,1)}, bf16[4096,128]{1,0:T(8,128)(2,1)}, bf16[4096,128]{1,0:T(8,128)(2,1)}, bf16[4096,128]{1,0:T(8,128)(2,1)}) custom-call(bf16[4096,128]{1,0:T(8,128)(2,1)S(1)} %copy-done, bf16[4096,128]{1,0:T(8,128)(2,1)S(1)} %copy-done.1, bf16[4096,128]{1,0:T(8,128)(2,1)S(1)} %copy-done.2, bf16[4096,128]{1,0:T(8,128)(2,1)S(1)} %copy-done.3, ...), custom_call_target="tpu_custom_call" | custom-call | flops 5242880 | bytes 10485760 | tf_op jit(solution)/shard_map/finish/pallas_call | solution.py:334
  (7 shorter events, 0.0 us)
Async XLA Ops:
  3.9 41.1 %all-to-all-start = ((bf16[128,64,128]{2,1,0:T(8,128)(2,1)}), bf16[128,64,128]{2,1,0:T(8,128)(2,1)S(1)}, u32[]{:S(2)}, u32[]{:S(2)}) async-start(bf16[128,64,128]{2,1,0:T(8,128)(2,1)} %products.1), calls=%async_computation | async-start | bytes 4194304 | tf_op jit(solution)/shard_map/all_to_all | solution.py:349
  15.0 29.9 %copy-start.5 = (bf16[256,256]{1,0:T(8,128)(2,1)S(1)}, bf16[256,256]{1,0:T(8,128)(2,1)}, u32[]{:S(2)}) copy-start(bf16[256,256]{1,0:T(8,128)(2,1)} %constant.31.clone.gather_lo) | copy-start | bytes 393220
  15.0 29.9 %copy-start.6 = (bf16[256,256]{1,0:T(8,128)(2,1)S(1)}, bf16[256,256]{1,0:T(8,128)(2,1)}, u32[]{:S(2)}) copy-start(bf16[256,256]{1,0:T(8,128)(2,1)} %constant.30.clone.gather_hi) | copy-start | bytes 393220
  15.0 29.9 %copy-start.7 = (bf16[256,256]{1,0:T(8,128)(2,1)S(1)}, bf16[256,256]{1,0:T(8,128)(2,1)}, u32[]{:S(2)}) copy-start(bf16[256,256]{1,0:T(8,128)(2,1)} %constant.29.clone.spread_lo) | copy-start | bytes 393220
  15.1 29.9 %copy-start.8 = (bf16[256,256]{1,0:T(8,128)(2,1)S(1)}, bf16[256,256]{1,0:T(8,128)(2,1)}, u32[]{:S(2)}) copy-start(bf16[256,256]{1,0:T(8,128)(2,1)} %constant.28.clone.spread_hi) | copy-start | bytes 393220
  15.1 29.9 %copy-start.9 = (bf16[256,256]{1,0:T(8,128)(2,1)S(1)}, bf16[256,256]{1,0:T(8,128)(2,1)}, u32[]{:S(2)}) copy-start(bf16[256,256]{1,0:T(8,128)(2,1)} %constant.24.clone.fold) | copy-start | bytes 393220
  15.1 29.9 %copy-start.10 = (f32[128,128]{1,0:T(8,128)S(1)}, f32[128,128]{1,0:T(8,128)}, u32[]{:S(2)}) copy-start(f32[128,128]{1,0:T(8,128)} %constant.27.clone.turn_im) | copy-start | bytes 196612
  15.1 29.9 %copy-start.11 = (f32[128,128]{1,0:T(8,128)S(1)}, f32[128,128]{1,0:T(8,128)}, u32[]{:S(2)}) copy-start(f32[128,128]{1,0:T(8,128)} %constant.26.clone.turn_re) | copy-start | bytes 196612
  15.1 29.9 %copy-start.12 = (bf16[128,256]{1,0:T(8,128)(2,1)S(1)}, bf16[128,256]{1,0:T(8,128)(2,1)}, u32[]{:S(2)}) copy-start(bf16[128,256]{1,0:T(8,128)(2,1)} %constant.33.clone.unfold_lo) | copy-start | bytes 196612
  15.1 29.9 %copy-start.13 = (bf16[128,256]{1,0:T(8,128)(2,1)S(1)}, bf16[128,256]{1,0:T(8,128)(2,1)}, u32[]{:S(2)}) copy-start(bf16[128,256]{1,0:T(8,128)(2,1)} %constant.32.clone.unfold_hi) | copy-start | bytes 196612
  56.1 35.3 %all-to-all-start.1 = ((bf16[128,64,128]{2,1,0:T(8,128)(2,1)}), bf16[128,64,128]{2,1,0:T(8,128)(2,1)}, u32[]{:S(2)}, u32[]{:S(2)}) async-start(bf16[128,64,128]{2,1,0:T(8,128)(2,1)} %get-tuple-element.13), calls=%async_computation.1 | async-start | bytes 4194304 | tf_op jit(solution)/shard_map/all_to_all | solution.py:349
  62.5 28.9 %copy-start = (bf16[4096,128]{1,0:T(8,128)(2,1)S(1)}, bf16[4096,128]{1,0:T(8,128)(2,1)}, u32[]{:S(2)}) copy-start(bf16[4096,128]{1,0:T(8,128)(2,1)} %query.3) | copy-start | bytes 3145732
  62.5 28.9 %copy-start.1 = (bf16[4096,128]{1,0:T(8,128)(2,1)S(1)}, bf16[4096,128]{1,0:T(8,128)(2,1)}, u32[]{:S(2)}) copy-start(bf16[4096,128]{1,0:T(8,128)(2,1)} %key_in.3) | copy-start | bytes 3145732
  62.6 28.9 %copy-start.2 = (bf16[4096,128]{1,0:T(8,128)(2,1)S(1)}, bf16[4096,128]{1,0:T(8,128)(2,1)}, u32[]{:S(2)}) copy-start(bf16[4096,128]{1,0:T(8,128)(2,1)} %value_in.3) | copy-start | bytes 3145732
  62.6 28.9 %copy-start.4 = (f32[4096]{0:T(1024)S(1)}, f32[4096]{0:T(1024)}, u32[]{:S(2)}) copy-start(f32[4096]{0:T(1024)} %param.20) | copy-start | bytes 49156
  91.4 1.2 %copy-start.3 = (bf16[4096,128]{1,0:T(8,128)(2,1)S(1)}, bf16[4096,128]{1,0:T(8,128)(2,1)}, u32[]{:S(2)}) copy-start(bf16[4096,128]{1,0:T(8,128)(2,1)} %cotangent.3) | copy-start | bytes 3145732

commit v3 on v2

--- a/solution.py
+++ b/solution.py
@@ -11,6 +11,7 @@
 F32 = jnp.float32
 BF16 = jnp.bfloat16
 SIDE = 128
+TILT = 1.62305
 GROUP = 8
 OCTET = 8
 
@@ -19,6 +20,12 @@
     high = np.asarray(values, np.float32).astype(BF16)
     low = (values - high.astype(np.float64)).astype(np.float32).astype(BF16)
     return high, low
+
+
+def one_term(values):
+    high = (values * TILT).astype(np.float32).astype(BF16)
+    wide = high.astype(np.float64)
+    return high, float((wide * values).sum() / (values * values).sum())
 
 
 def tables():
@@ -31,7 +38,11 @@
     fold_hi, fold_lo = two_terms(fold)
     spread_hi, spread_lo = two_terms(np.block([[cos_t, -sin_t], [sin_t, cos_t]]))
     gather_hi, gather_lo = two_terms(np.block([[cos_t, sin_t], [-sin_t, cos_t]]) / SIDE)
-    unfold_hi, unfold_lo = two_terms(np.concatenate([np.cos(psi), -np.sin(psi)], axis=1) / SIDE)
+    unfold = np.concatenate([np.cos(psi), -np.sin(psi)], axis=1) / SIDE
+    unfold_hi, unfold_lo = two_terms(unfold)
+    spread_one, spread_gain = one_term(np.block([[cos_t, -sin_t], [sin_t, cos_t]]))
+    gather_one, gather_gain = one_term(np.block([[cos_t, sin_t], [-sin_t, cos_t]]) / SIDE)
+    level_hi, level_lo = two_terms(unfold / (spread_gain * gather_gain))
     return dict(
         fold=np.concatenate([fold_hi, fold_lo], axis=1),
         fold_hi=fold_hi,
@@ -40,6 +51,8 @@
         spread_hi=spread_hi, spread_lo=spread_lo,
         gather_hi=gather_hi, gather_lo=gather_lo,
         unfold_hi=unfold_hi, unfold_lo=unfold_lo,
+        spread_one=spread_one, gather_one=gather_one,
+        level_hi=level_hi, level_lo=level_lo, cross_gain=spread_gain**2,
     )
 
 
@@ -99,6 +112,9 @@
 def times_rows(hi, lo, store, c, passes):
     rows = pl.ds(c * 2 * SIDE, 2 * SIDE)
     high = store[0, rows, :]
+    if passes == 2:
+        both = dot(join([hi[...], lo[...]], 0), high)
+        return both[:SIDE] + both[SIDE:]
     lhs, rhs = [hi[...]], [high]
     if passes >= 2:
         lhs, rhs = lhs + [lo[...]], rhs + [high]
@@ -132,34 +148,54 @@
         target[:, o * OCTET:(o + 2) * OCTET, :] = pair.astype(BF16)
 
 
-def signal_kernel(passes, got, fil, fold, turn_re, turn_im, spread_hi, spread_lo, gather_hi, gather_lo, unfold_hi, unfold_lo,
-                  send, cross, skip, stage, result, turned, product, tilted):
+def signal_kernel(got, fil, fold, turn_re, turn_im, spread, gather, unfold_hi, unfold_lo,
+                  send, cross, skip, spectra, stage, result, turned, product, tilted, crossed, packed, fil_sem, cross_sem, send_sem):
     rows = 2 * GROUP
-    load_octets(got, stage)
-    tr, ti = turn_re, turn_im
-    for c in range(GROUP):
-        mix = stage[c // OCTET, pl.ds(c % OCTET, SIDE, stride=OCTET), :]
-        wgt = stage[(c + GROUP) // OCTET, pl.ds((c + GROUP) % OCTET, SIDE, stride=OCTET), :]
-        skip[c:c + 1, :] = jnp.sum(mix * wgt, axis=0, keepdims=True)
-        keep(turned, c, turn_folded(fold_pair(join([mix, wgt], 1), True, fold, None), tr, ti), passes[0])
-    for c in range(GROUP):
-        both = rows_times(turned, c, spread_hi, spread_lo, passes[0])
-        mr, mi = both[:SIDE, :SIDE], both[:SIDE, SIDE:]
-        wr, wi = both[SIDE:, :SIDE], both[SIDE:, SIDE:]
-        fr, fi = fil[0, c, :, :SIDE], fil[0, c, :, SIDE:]
-        cross[0, c, :, :SIDE] = (wr * mr + wi * mi).astype(BF16)
-        cross[0, c, :, SIDE:] = (wi * mr - wr * mi).astype(BF16)
-        keep(product, c, join([
-            join([fr * mr - fi * mi, fr * mi + fi * mr], 1),
-            join([fr * wr + fi * wi, fr * wi - fi * wr], 1),
-        ], 0), passes[1])
-    for c in range(GROUP):
-        keep(tilted, c, turn_back(rows_times(product, c, gather_hi, gather_lo, passes[1]), tr, ti), passes[2])
-    for c in range(GROUP):
-        back = times_rows(unfold_hi, unfold_lo, tilted, c, passes[2])
-        result[c // OCTET, pl.ds(c % OCTET, SIDE, stride=OCTET), :] = back[:, :SIDE]
-        result[(c + GROUP) // OCTET, pl.ds((c + GROUP) % OCTET, SIDE, stride=OCTET), :] = back[:, SIDE:]
-    store_octets(result, send)
+    groups = spectra.shape[0]
+
+    def fetch(g):
+        return pltpu.make_async_copy(fil.at[g], spectra.at[g], fil_sem.at[g])
+
+    def put(g):
+        return (pltpu.make_async_copy(crossed.at[g], cross.at[g], cross_sem.at[g]),
+                pltpu.make_async_copy(packed.at[g], send.at[:, pl.ds(pl.multiple_of(g * rows, rows), rows), :], send_sem.at[g]))
+
+    for g in range(groups):
+        fetch(g).start()
+
+    @pl.loop(0, groups)
+    def _(g):
+        fetch(g).wait()
+        load_octets(got.at[:, pl.ds(pl.multiple_of(g * rows, rows), rows), :], stage)
+        for c in range(GROUP):
+            mix = stage[c // OCTET, pl.ds(c % OCTET, SIDE, stride=OCTET), :]
+            wgt = stage[(c + GROUP) // OCTET, pl.ds((c + GROUP) % OCTET, SIDE, stride=OCTET), :]
+            skip[g, c:c + 1, :] = jnp.sum(mix * wgt, axis=0, keepdims=True)
+            keep(turned, c, turn_folded(fold_pair(join([mix, wgt], 1), True, fold, None), turn_re, turn_im), 1)
+        for c in range(GROUP):
+            both = rows_times(turned, c, spread, None, 1)
+            mr, mi = both[:SIDE, :SIDE], both[:SIDE, SIDE:]
+            wr, wi = both[SIDE:, :SIDE], both[SIDE:, SIDE:]
+            fr, fi = spectra[g, c, :, :SIDE], spectra[g, c, :, SIDE:]
+            crossed[g, c, :, :SIDE] = (wr * mr + wi * mi).astype(BF16)
+            crossed[g, c, :, SIDE:] = (wi * mr - wr * mi).astype(BF16)
+            keep(product, c, join([
+                join([fr * mr - fi * mi, fr * mi + fi * mr], 1),
+                join([fr * wr + fi * wi, fr * wi - fi * wr], 1),
+            ], 0), 1)
+        for c in range(GROUP):
+            keep(tilted, c, turn_back(rows_times(product, c, gather, None, 1), turn_re, turn_im), 2)
+        for c in range(GROUP):
+            back = times_rows(unfold_hi, unfold_lo, tilted, c, 2)
+            result[c // OCTET, pl.ds(c % OCTET, SIDE, stride=OCTET), :] = back[:, :SIDE]
+            result[(c + GROUP) // OCTET, pl.ds((c + GROUP) % OCTET, SIDE, stride=OCTET), :] = back[:, SIDE:]
+        store_octets(result, packed.at[g])
+        for copy in put(g):
+            copy.start()
+
+    for g in range(groups):
+        for copy in put(g):
+            copy.wait()
 
 
 def grad_kernel(scale, cross, turn_re, turn_im, gather_hi, gather_lo, unfold_hi, unfold_lo, out, stage, tilted):
@@ -218,20 +254,18 @@
 def convolve(got, spec, tab, passes):
     groups = spec.shape[0]
     channels = groups * GROUP
-    ops = [tab[k] for k in ("fold", "turn_re", "turn_im", "spread_hi", "spread_lo", "gather_hi", "gather_lo", "unfold_hi", "unfold_lo")]
+    ops = [tab[k] for k in ("fold", "turn_re", "turn_im", "spread_one", "gather_one", "level_hi", "level_lo")]
     rows = 2 * GROUP
     return pl.pallas_call(
-        functools.partial(signal_kernel, passes),
-        grid=(groups,),
-        in_specs=[pl.BlockSpec((SIDE, rows, SIDE), lambda g: (0, g, 0)),
-                  pl.BlockSpec((1, GROUP, SIDE, 2 * SIDE), lambda g: (g, 0, 0, 0))] + [whole(o) for o in ops],
-        out_specs=[pl.BlockSpec((SIDE, rows, SIDE), lambda g: (0, g, 0)),
-                   pl.BlockSpec((1, GROUP, SIDE, 2 * SIDE), lambda g: (g, 0, 0, 0)),
-                   pl.BlockSpec((GROUP, SIDE), lambda g: (g, 0))],
+        signal_kernel,
+        in_specs=[NEAR, FAR] + [NEAR] * len(ops),
+        out_specs=[FAR, FAR, NEAR],
         out_shape=[pltpu.HBM((SIDE, 2 * channels, SIDE), BF16),
                    pltpu.HBM(spec.shape, BF16),
-                   jax.ShapeDtypeStruct((channels, SIDE), F32)],
-        scratch_shapes=[pltpu.VMEM((rows // OCTET, SIDE * OCTET, SIDE), F32)] * 2 + [held(2 * GROUP)] * 3,
+                   jax.ShapeDtypeStruct((groups, GROUP, SIDE), F32)],
+        scratch_shapes=[pltpu.VMEM(spec.shape, F32)] + [pltpu.VMEM((rows // OCTET, SIDE * OCTET, SIDE), F32)] * 2 + [held(2 * GROUP)] * 3
+        + [pltpu.VMEM(spec.shape, BF16), pltpu.VMEM((groups, SIDE, rows, SIDE), BF16)]
+        + [pltpu.SemaphoreType.DMA((groups,))] * 3,
         compiler_params=granted(48),
         cost_estimate=cost(channels * 17 * SIDE, 12 * channels * SIDE * SIDE),
         name="convolve",
@@ -243,7 +277,7 @@
     channels = groups * GROUP
     ops = [tab[k] for k in ("turn_re", "turn_im", "gather_hi", "gather_lo", "unfold_hi", "unfold_lo")]
     return pl.pallas_call(
-        functools.partial(grad_kernel, scale),
+        functools.partial(grad_kernel, scale / tab["cross_gain"]),
         grid=(groups,),
         in_specs=[pl.BlockSpec((1, GROUP, SIDE, 2 * SIDE), lambda g: (g, 0, 0, 0))] + [whole(o) for o in ops],
         out_specs=pl.BlockSpec((GROUP, SIDE * SIDE), lambda g: (g, 0)),
@@ -302,9 +336,9 @@
 
 
 def finish_kernel(query, key_in, value_in, cotangent, got, gain, output, grad_query, grad_key, grad_value,
-                  c, both, spread, out_a, out_b, out_c, out_d, in_sem, out_sem):
+                  k, v, c, spread, out_a, out_b, out_c, out_d, in_sem, out_sem):
     results = (out_a, out_b, out_c, out_d)
-    loads = fetches((cotangent, got), (c, both), in_sem)
+    loads = fetches((key_in, value_in, cotangent), (k, v, c), in_sem)
     stores = fetches(results, (output, grad_query, grad_key, grad_value), out_sem)
     for group in loads:
         for copy in group:
@@ -314,7 +348,7 @@
     for i in range(PIECES):
         for copy in loads[i]:
             copy.wait()
-        qi, ki, vi, ci, pair = [chunk(x, i)[...].astype(F32) for x in (query, key_in, value_in, c, both)]
+        qi, ki, vi, ci, pair = [chunk(x, i)[...].astype(F32) for x in (query, k, v, c, got)]
         pair = pair.reshape(-1, 2, GROUP, SIDE)
         conv, back = pair[:, 0].reshape(qi.shape), pair[:, 1].reshape(qi.shape)
         g = chunk(spread, i)[...]
@@ -333,16 +367,20 @@
     channels = query.shape[0]
     return pl.pallas_call(
         finish_kernel,
-        in_specs=[NEAR] * 3 + [FAR] * 2 + [NEAR],
+        in_specs=[NEAR] + [FAR] * 3 + [NEAR] * 2,
         out_specs=[FAR] * 4,
         out_shape=[jax.ShapeDtypeStruct(query.shape, BF16)] * 4,
-        scratch_shapes=[pltpu.VMEM(query.shape, BF16), pltpu.VMEM(got.shape, BF16), pltpu.VMEM(query.shape, F32)]
+        scratch_shapes=[pltpu.VMEM(query.shape, BF16)] * 3 + [pltpu.VMEM(query.shape, F32)]
         + [pltpu.VMEM(query.shape, BF16)] * 4
-        + [pltpu.SemaphoreType.DMA((2, PIECES)), pltpu.SemaphoreType.DMA((4, PIECES))],
+        + [pltpu.SemaphoreType.DMA((3, PIECES)), pltpu.SemaphoreType.DMA((4, PIECES))],
         compiler_params=granted(48),
         cost_estimate=pl.CostEstimate(flops=10 * channels * SIDE, bytes_accessed=20 * channels * SIDE, transcendentals=0),
         name="finish",
     )(query, key_in, value_in, cotangent, got, gain)
+
+
+def far(array):
+    return pltpu.with_memory_space_constraint(array, pltpu.HBM)
 
 
 def exchange(blocks):
@@ -355,11 +393,11 @@
     got = exchange(products(query, key_in, value_in, cotangent, filters.shape[0]))
     spec = filter_spectra(filters, tab)
     gain = skip_gain.reshape(-1, SIDE)
-    send, cross, skip = convolve(got, spec, tab, (2, 2, 2))
+    send, cross, skip = convolve(got, spec, tab, (1, 1, 2))
     back = exchange(send)
     grad_filters = filter_gradient(cross, tab, scale)
     grad_skip = jnp.sum(skip.reshape(-1, SIDE), axis=1) * scale
-    return (*finish(query, key_in, value_in, cotangent, back, gain), grad_filters, grad_skip)
+    return (*finish(query, far(key_in), far(value_in), far(cotangent), back, gain), grad_filters, grad_skip)
 
 
 def solution(mesh):

time: 96.9 us -> 93.8 us (0.968)
  Pallas kernels: 30.5 us -> 29.1 us
    pallas_call x3, Pallas kernels: 20.6 us -> 19.3 us  [the longest x1 9.37 us: convolve(): pl.pallas_call(signal_kernel, in_specs=[NEAR, FAR] + [NEAR] * len(ops), o...]
    unnamed x28 -> x18, local copies, waits for them, and re-layouts: 1.3 us -> 0.06 us
where the time goes in v3:
time: 93.8 us; the launch traced here: 93.4 us
  waiting for transfers between devices  46.7 us (50%)
  Pallas kernels  29.1 us (31%)
  starting transfers between devices  16 us (17%)
    all_to_all x2, waiting for transfers between devices, exchange(): lax.all_to_all(blocks, ('node', 'local'), split_axis=0, concat_axis=0, ti...  46.7 us
    all_to_all x2, starting transfers between devices, exchange(): lax.all_to_all(blocks, ('node', 'local'), split_axis=0, concat_axis=0, ti...  16 us
    pallas_call x1, Pallas kernels, convolve(): pl.pallas_call(signal_kernel, in_specs=[NEAR, FAR] + [NEAR] * len(ops), o...  9.37 us
    pallas_call x1, Pallas kernels, filter_spectra(): pl.pallas_call(filter_kernel, grid=(groups,), in_specs=[pl.BlockSpec((GRO...  6.65 us
    pallas_call x1, Pallas kernels, filter_gradient(): pl.pallas_call(functools.partial(grad_kernel, scale / tab['cross_gain']),...  5.7 us
    pallas_call x1, Pallas kernels, finish(): pl.pallas_call(finish_kernel, in_specs=[NEAR] + [FAR] * 3 + [NEAR] * 2, o...  4.19 us
    pallas_call x1, Pallas kernels, products(): pl.pallas_call(products_kernel, in_specs=[FAR] * 4, out_specs=FAR, out_sh...  3.23 us
  transfers between devices with their start and end apart: 2, of which 2 were waited for; matrix products, arithmetic and copies ran while one was open for 1% of the time, Pallas kernels for 13%

profile of v3, /device:TPU:0, one launch (start us, length us, event | category | flops | bytes accessed | tf_op | source)
XLA Modules:
  0.0 93.4 jit_solution(1701845478819583212)
XLA Ops:
  0.6 3.2 %products.1 = bf16[128,64,128]{2,1,0:T(8,128)(2,1)} custom-call(bf16[4096,128]{1,0:T(8,128)(2,1)} %query.3, bf16[4096,128]{1,0:T(8,128)(2,1)} %key_in.3, bf16[4096,128]{1,0:T(8,128)(2,1)} %value_in.3, bf16[4096,128]{1,0:T(8,128)(2,1)} %cotangent.3), custom_call_target="tpu_custom_call" | custom-call | flops 1048576 | bytes 6291456 | tf_op jit(solution)/shard_map/products/pallas_call | solution.py:325
  3.9 11.1 %all-to-all-start = ((bf16[128,64,128]{2,1,0:T(8,128)(2,1)}), bf16[128,64,128]{2,1,0:T(8,128)(2,1)S(1)}, u32[]{:S(2)}, u32[]{:S(2)}) async-start(bf16[128,64,128]{2,1,0:T(8,128)(2,1)} %products.1), calls=%async_computation | async-start | bytes 4194304 | tf_op jit(solution)/shard_map/all_to_all | solution.py:387
  15.0 0.0 copy-start.2
  15.0 0.0 copy-start.3
  15.0 0.0 copy-start.4
  15.1 0.0 copy-start.5
  15.1 0.0 copy-start.6
  15.1 0.0 copy-start.7
  15.1 0.0 copy-start.8
  15.1 6.6 %filter_spectra.1.fil = f32[4,8,128,256]{3,2,1,0:T(8,128)} custom-call(f32[32,16384]{1,0:T(8,128)} %fil.1, bf16[256,256]{1,0:T(8,128)(2,1)} %constant.32.clone.fold, bf16[256,128]{1,0:T(8,128)(2,1)} %constant.33.clone.fold_hi, f32[128,128]{1,0:T(8,128)} %constant.34.clone.turn_re, f32[128,128]{1,0:T(8,128)} %constant.35.clone.turn_im, ...), custom_call_target="tpu_custom_call" | custom-call | flops 2684354560 | bytes 6291456 | tf_op jit(solution)/shard_map/filter_spectra/pallas_call | solution.py:241
  21.8 23.2 %all-to-all-done.got = bf16[128,64,128]{2,1,0:T(8,128)(2,1)S(1)} async-done(((bf16[128,64,128]{2,1,0:T(8,128)(2,1)}), bf16[128,64,128]{2,1,0:T(8,128)(2,1)S(1)}, u32[]{:S(2)}, u32[]{:S(2)}) %all-to-all-start) | async-done | bytes 2097184 | tf_op jit(solution)/shard_map/all_to_all | solution.py:387
  45.0 0.0 copy-done.2
  45.0 0.0 copy-done.3
  45.0 0.0 copy-done.4
  45.0 0.0 copy-done.5
  45.0 0.0 copy-done.6
  45.0 0.0 copy-done.7
  45.0 0.0 copy-done.8
  45.0 9.4 %convolve.1 = (bf16[128,64,128]{2,1,0:T(8,128)(2,1)}, bf16[4,8,128,256]{3,2,1,0:T(8,128)(2,1)}, f32[4,8,128]{2,1,0:T(8,128)S(1)}) custom-call(bf16[128,64,128]{2,1,0:T(8,128)(2,1)S(1)} %all-to-all-done.got, f32[4,8,128,256]{3,2,1,0:T(8,128)} %filter_spectra.1.fil, bf16[256,256]{1,0:T(8,128)(2,1)S(1)} %copy-done.2, f32[128,128]{1,0:T(8,128)S(1)} %copy-done.6, ...), custom_call_target="tpu_custom_call" | custom-call | flops 9126805504 | bytes 6291456 | tf_op jit(solution)/shard_map/convolve/pallas_call | solution.py:259
  54.4 4.9 %all-to-all-start.1 = ((bf16[128,64,128]{2,1,0:T(8,128)(2,1)}), bf16[128,64,128]{2,1,0:T(8,128)(2,1)S(1)}, u32[]{:S(2)}, u32[]{:S(2)}) async-start(bf16[128,64,128]{2,1,0:T(8,128)(2,1)} %get-tuple-element.13), calls=%async_computation.1 | async-start | bytes 4194304 | tf_op jit(solution)/shard_map/all_to_all | solution.py:387
  59.3 0.1 reduce_sum.9
  59.4 0.6 mul.11
  60.0 0.0 copy-start
  60.0 0.0 copy-start.1
  60.0 5.7 %filter_gradient.1 = f32[32,16384]{1,0:T(8,128)} custom-call(bf16[4,8,128,256]{3,2,1,0:T(8,128)(2,1)} %get-tuple-element.18.cross, f32[128,128]{1,0:T(8,128)} %constant.34.clone.turn_re, f32[128,128]{1,0:T(8,128)} %constant.35.clone.turn_im, bf16[256,256]{1,0:T(8,128)(2,1)} %constant.42.clone.gather_hi, bf16[256,256]{1,0:T(8,128)(2,1)} %constant.43.clone.gather_lo, ...), custom_call_target="tpu_custom_call" | custom-call | flops 2684354560 | bytes 6291456 | tf_op jit(solution)/shard_map/filter_gradient/pallas_call | solution.py:279
  65.7 23.5 %all-to-all-done.1.got = bf16[128,64,128]{2,1,0:T(8,128)(2,1)S(1)} async-done(((bf16[128,64,128]{2,1,0:T(8,128)(2,1)}), bf16[128,64,128]{2,1,0:T(8,128)(2,1)S(1)}, u32[]{:S(2)}, u32[]{:S(2)}) %all-to-all-start.1) | async-done | bytes 2097184 | tf_op jit(solution)/shard_map/all_to_all | solution.py:387
  89.2 0.0 copy-done
  89.2 0.0 copy-done.1
  89.2 4.2 %finish.1 = (bf16[4096,128]{1,0:T(8,128)(2,1)}, bf16[4096,128]{1,0:T(8,128)(2,1)}, bf16[4096,128]{1,0:T(8,128)(2,1)}, bf16[4096,128]{1,0:T(8,128)(2,1)}) custom-call(bf16[4096,128]{1,0:T(8,128)(2,1)S(1)} %copy-done, bf16[4096,128]{1,0:T(8,128)(2,1)} %key_in.3, bf16[4096,128]{1,0:T(8,128)(2,1)} %value_in.3, bf16[4096,128]{1,0:T(8,128)(2,1)} %cotangent.3, ...), custom_call_target="tpu_custom_call" | custom-call | flops 5242880 | bytes 10485760 | tf_op jit(solution)/shard_map/finish/pallas_call | solution.py:368
  (1 shorter events, 0.0 us)
Async XLA Ops:
  3.9 41.1 %all-to-all-start = ((bf16[128,64,128]{2,1,0:T(8,128)(2,1)}), bf16[128,64,128]{2,1,0:T(8,128)(2,1)S(1)}, u32[]{:S(2)}, u32[]{:S(2)}) async-start(bf16[128,64,128]{2,1,0:T(8,128)(2,1)} %products.1), calls=%async_computation | async-start | bytes 4194304 | tf_op jit(solution)/shard_map/all_to_all | solution.py:387
  15.0 29.9 %copy-start.2 = (bf16[256,256]{1,0:T(8,128)(2,1)S(1)}, bf16[256,256]{1,0:T(8,128)(2,1)}, u32[]{:S(2)}) copy-start(bf16[256,256]{1,0:T(8,128)(2,1)} %constant.32.clone.fold) | copy-start | bytes 393220
  15.0 29.9 %copy-start.3 = (bf16[256,256]{1,0:T(8,128)(2,1)S(1)}, bf16[256,256]{1,0:T(8,128)(2,1)}, u32[]{:S(2)}) copy-start(bf16[256,256]{1,0:T(8,128)(2,1)} %constant.39.clone.gather) | copy-start | bytes 393220
  15.0 29.9 %copy-start.4 = (bf16[256,256]{1,0:T(8,128)(2,1)S(1)}, bf16[256,256]{1,0:T(8,128)(2,1)}, u32[]{:S(2)}) copy-start(bf16[256,256]{1,0:T(8,128)(2,1)} %constant.38.clone.spread) | copy-start | bytes 393220
  15.1 29.9 %copy-start.5 = (f32[128,128]{1,0:T(8,128)S(1)}, f32[128,128]{1,0:T(8,128)}, u32[]{:S(2)}) copy-start(f32[128,128]{1,0:T(8,128)} %constant.35.clone.turn_im) | copy-start | bytes 196612
  15.1 29.9 %copy-start.6 = (f32[128,128]{1,0:T(8,128)S(1)}, f32[128,128]{1,0:T(8,128)}, u32[]{:S(2)}) copy-start(f32[128,128]{1,0:T(8,128)} %constant.34.clone.turn_re) | copy-start | bytes 196612
  15.1 29.9 %copy-start.7 = (bf16[128,256]{1,0:T(8,128)(2,1)S(1)}, bf16[128,256]{1,0:T(8,128)(2,1)}, u32[]{:S(2)}) copy-start(bf16[128,256]{1,0:T(8,128)(2,1)} %constant.41.clone.unfold_lo) | copy-start | bytes 196612
  15.1 29.9 %copy-start.8 = (bf16[128,256]{1,0:T(8,128)(2,1)S(1)}, bf16[128,256]{1,0:T(8,128)(2,1)}, u32[]{:S(2)}) copy-start(bf16[128,256]{1,0:T(8,128)(2,1)} %constant.40.clone.unfold_hi) | copy-start | bytes 196612
  54.4 34.8 %all-to-all-start.1 = ((bf16[128,64,128]{2,1,0:T(8,128)(2,1)}), bf16[128,64,128]{2,1,0:T(8,128)(2,1)S(1)}, u32[]{:S(2)}, u32[]{:S(2)}) async-start(bf16[128,64,128]{2,1,0:T(8,128)(2,1)} %get-tuple-element.13), calls=%async_computation.1 | async-start | bytes 4194304 | tf_op jit(solution)/shard_map/all_to_all | solution.py:387
  60.0 29.2 %copy-start = (bf16[4096,128]{1,0:T(8,128)(2,1)S(1)}, bf16[4096,128]{1,0:T(8,128)(2,1)}, u32[]{:S(2)}) copy-start(bf16[4096,128]{1,0:T(8,128)(2,1)} %query.3) | copy-start | bytes 3145732
  60.0 29.2 %copy-start.1 = (f32[4096]{0:T(1024)S(1)}, f32[4096]{0:T(1024)}, u32[]{:S(2)}) copy-start(f32[4096]{0:T(1024)} %param.24) | copy-start | bytes 49156

commit v4 on v3

--- a/solution.py
+++ b/solution.py
@@ -158,20 +158,22 @@
 
     def put(g):
         return (pltpu.make_async_copy(crossed.at[g], cross.at[g], cross_sem.at[g]),
-                pltpu.make_async_copy(packed.at[g], send.at[:, pl.ds(pl.multiple_of(g * rows, rows), rows), :], send_sem.at[g]))
+                pltpu.make_async_copy(packed.at[g], send.at[:, pl.ds(g * rows, rows), :], send_sem.at[g]))
 
     for g in range(groups):
         fetch(g).start()
 
-    @pl.loop(0, groups)
-    def _(g):
-        fetch(g).wait()
-        load_octets(got.at[:, pl.ds(pl.multiple_of(g * rows, rows), rows), :], stage)
+    for g in range(groups):
+        if g > 0:
+            fetch(g).wait()
+        load_octets(got.at[:, pl.ds(g * rows, rows), :], stage)
         for c in range(GROUP):
             mix = stage[c // OCTET, pl.ds(c % OCTET, SIDE, stride=OCTET), :]
             wgt = stage[(c + GROUP) // OCTET, pl.ds((c + GROUP) % OCTET, SIDE, stride=OCTET), :]
             skip[g, c:c + 1, :] = jnp.sum(mix * wgt, axis=0, keepdims=True)
             keep(turned, c, turn_folded(fold_pair(join([mix, wgt], 1), True, fold, None), turn_re, turn_im), 1)
+        if g == 0:
+            fetch(g).wait()
         for c in range(GROUP):
             both = rows_times(turned, c, spread, None, 1)
             mr, mi = both[:SIDE, :SIDE], both[:SIDE, SIDE:]
@@ -183,6 +185,9 @@
                 join([fr * mr - fi * mi, fr * mi + fi * mr], 1),
                 join([fr * wr + fi * wi, fr * wi - fi * wr], 1),
             ], 0), 1)
+        cross_out, send_out = put(g)
+        if g == groups - 1:
+            cross_out.start()
         for c in range(GROUP):
             keep(tilted, c, turn_back(rows_times(product, c, gather, None, 1), turn_re, turn_im), 2)
         for c in range(GROUP):
@@ -190,8 +195,9 @@
             result[c // OCTET, pl.ds(c % OCTET, SIDE, stride=OCTET), :] = back[:, :SIDE]
             result[(c + GROUP) // OCTET, pl.ds((c + GROUP) % OCTET, SIDE, stride=OCTET), :] = back[:, SIDE:]
         store_octets(result, packed.at[g])
-        for copy in put(g):
-            copy.start()
+        if g < groups - 1:
+            cross_out.start()
+        send_out.start()
 
     for g in range(groups):
         for copy in put(g):

time: 93.8 us -> 93.6 us (level)
  no operation moved by 1% of the time
where the time goes in v4:
time: 93.6 us; the launch traced here: 93.2 us
  waiting for transfers between devices  46.5 us (50%)
  Pallas kernels  28.8 us (31%)
  starting transfers between devices  16.2 us (17%)
    all_to_all x2, waiting for transfers between devices, exchange(): lax.all_to_all(blocks, ('node', 'local'), split_axis=0, concat_axis=0, ti...  46.5 us
    all_to_all x2, starting transfers between devices, exchange(): lax.all_to_all(blocks, ('node', 'local'), split_axis=0, concat_axis=0, ti...  16.2 us
    pallas_call x1, Pallas kernels, convolve(): pl.pallas_call(signal_kernel, in_specs=[NEAR, FAR] + [NEAR] * len(ops), o...  9 us
    pallas_call x1, Pallas kernels, filter_spectra(): pl.pallas_call(filter_kernel, grid=(groups,), in_specs=[pl.BlockSpec((GRO...  6.65 us
    pallas_call x1, Pallas kernels, filter_gradient(): pl.pallas_call(functools.partial(grad_kernel, scale / tab['cross_gain']),...  5.7 us
    pallas_call x1, Pallas kernels, finish(): pl.pallas_call(finish_kernel, in_specs=[NEAR] + [FAR] * 3 + [NEAR] * 2, o...  4.19 us
    pallas_call x1, Pallas kernels, products(): pl.pallas_call(products_kernel, in_specs=[FAR] * 4, out_specs=FAR, out_sh...  3.23 us
  transfers between devices with their start and end apart: 2, of which 2 were waited for; matrix products, arithmetic and copies ran while one was open for 1% of the time, Pallas kernels for 13%

profile of v4, /device:TPU:0, one launch (start us, length us, event | category | flops | bytes accessed | tf_op | source)
XLA Modules:
  0.0 93.2 jit_solution(7953319119893902035)
XLA Ops:
  0.6 3.2 %products.1 = bf16[128,64,128]{2,1,0:T(8,128)(2,1)} custom-call(bf16[4096,128]{1,0:T(8,128)(2,1)} %query.3, bf16[4096,128]{1,0:T(8,128)(2,1)} %key_in.3, bf16[4096,128]{1,0:T(8,128)(2,1)} %value_in.3, bf16[4096,128]{1,0:T(8,128)(2,1)} %cotangent.3), custom_call_target="tpu_custom_call" | custom-call | flops 1048576 | bytes 6291456 | tf_op jit(solution)/shard_map/products/pallas_call | solution.py:331
  3.9 11.1 %all-to-all-start = ((bf16[128,64,128]{2,1,0:T(8,128)(2,1)}), bf16[128,64,128]{2,1,0:T(8,128)(2,1)S(1)}, u32[]{:S(2)}, u32[]{:S(2)}) async-start(bf16[128,64,128]{2,1,0:T(8,128)(2,1)} %products.1), calls=%async_computation | async-start | bytes 4194304 | tf_op jit(solution)/shard_map/all_to_all | solution.py:393
  15.0 0.0 copy-start.2
  15.0 0.0 copy-start.3
  15.0 0.0 copy-start.4
  15.1 0.0 copy-start.5
  15.1 0.0 copy-start.6
  15.1 0.0 copy-start.7
  15.1 0.0 copy-start.8
  15.1 6.6 %filter_spectra.1.fil = f32[4,8,128,256]{3,2,1,0:T(8,128)} custom-call(f32[32,16384]{1,0:T(8,128)} %fil.1, bf16[256,256]{1,0:T(8,128)(2,1)} %constant.32.clone.fold, bf16[256,128]{1,0:T(8,128)(2,1)} %constant.33.clone.fold_hi, f32[128,128]{1,0:T(8,128)} %constant.34.clone.turn_re, f32[128,128]{1,0:T(8,128)} %constant.35.clone.turn_im, ...), custom_call_target="tpu_custom_call" | custom-call | flops 2684354560 | bytes 6291456 | tf_op jit(solution)/shard_map/filter_spectra/pallas_call | solution.py:247
  21.8 23.2 %all-to-all-done.got = bf16[128,64,128]{2,1,0:T(8,128)(2,1)S(1)} async-done(((bf16[128,64,128]{2,1,0:T(8,128)(2,1)}), bf16[128,64,128]{2,1,0:T(8,128)(2,1)S(1)}, u32[]{:S(2)}, u32[]{:S(2)}) %all-to-all-start) | async-done | bytes 2097184 | tf_op jit(solution)/shard_map/all_to_all | solution.py:393
  45.0 0.0 copy-done.2
  45.0 0.0 copy-done.3
  45.0 0.0 copy-done.4
  45.0 0.0 copy-done.5
  45.0 0.0 copy-done.6
  45.0 0.0 copy-done.7
  45.0 0.0 copy-done.8
  45.0 9.0 %convolve.1 = (bf16[128,64,128]{2,1,0:T(8,128)(2,1)}, bf16[4,8,128,256]{3,2,1,0:T(8,128)(2,1)}, f32[4,8,128]{2,1,0:T(8,128)S(1)}) custom-call(bf16[128,64,128]{2,1,0:T(8,128)(2,1)S(1)} %all-to-all-done.got, f32[4,8,128,256]{3,2,1,0:T(8,128)} %filter_spectra.1.fil, bf16[256,256]{1,0:T(8,128)(2,1)S(1)} %copy-done.2, f32[128,128]{1,0:T(8,128)S(1)} %copy-done.6, ...), custom_call_target="tpu_custom_call" | custom-call | flops 9126805504 | bytes 6291456 | tf_op jit(solution)/shard_map/convolve/pallas_call | solution.py:265
  54.0 5.1 %all-to-all-start.1 = ((bf16[128,64,128]{2,1,0:T(8,128)(2,1)}), bf16[128,64,128]{2,1,0:T(8,128)(2,1)S(1)}, u32[]{:S(2)}, u32[]{:S(2)}) async-start(bf16[128,64,128]{2,1,0:T(8,128)(2,1)} %get-tuple-element.13), calls=%async_computation.1 | async-start | bytes 4194304 | tf_op jit(solution)/shard_map/all_to_all | solution.py:393
  59.1 0.1 reduce_sum.9
  59.2 0.6 mul.11
  59.8 0.0 copy-start
  59.8 0.0 copy-start.1
  59.8 5.7 %filter_gradient.1 = f32[32,16384]{1,0:T(8,128)} custom-call(bf16[4,8,128,256]{3,2,1,0:T(8,128)(2,1)} %get-tuple-element.18.cross, f32[128,128]{1,0:T(8,128)} %constant.34.clone.turn_re, f32[128,128]{1,0:T(8,128)} %constant.35.clone.turn_im, bf16[256,256]{1,0:T(8,128)(2,1)} %constant.42.clone.gather_hi, bf16[256,256]{1,0:T(8,128)(2,1)} %constant.43.clone.gather_lo, ...), custom_call_target="tpu_custom_call" | custom-call | flops 2684354560 | bytes 6291456 | tf_op jit(solution)/shard_map/filter_gradient/pallas_call | solution.py:285
  65.5 23.4 %all-to-all-done.1.got = bf16[128,64,128]{2,1,0:T(8,128)(2,1)S(1)} async-done(((bf16[128,64,128]{2,1,0:T(8,128)(2,1)}), bf16[128,64,128]{2,1,0:T(8,128)(2,1)S(1)}, u32[]{:S(2)}, u32[]{:S(2)}) %all-to-all-start.1) | async-done | bytes 2097184 | tf_op jit(solution)/shard_map/all_to_all | solution.py:393
  88.8 0.0 copy-done
  88.8 0.0 copy-done.1
  88.8 4.2 %finish.1 = (bf16[4096,128]{1,0:T(8,128)(2,1)}, bf16[4096,128]{1,0:T(8,128)(2,1)}, bf16[4096,128]{1,0:T(8,128)(2,1)}, bf16[4096,128]{1,0:T(8,128)(2,1)}) custom-call(bf16[4096,128]{1,0:T(8,128)(2,1)S(1)} %copy-done, bf16[4096,128]{1,0:T(8,128)(2,1)} %key_in.3, bf16[4096,128]{1,0:T(8,128)(2,1)} %value_in.3, bf16[4096,128]{1,0:T(8,128)(2,1)} %cotangent.3, ...), custom_call_target="tpu_custom_call" | custom-call | flops 5242880 | bytes 10485760 | tf_op jit(solution)/shard_map/finish/pallas_call | solution.py:374
  (1 shorter events, 0.0 us)
Async XLA Ops:
  3.9 41.1 %all-to-all-start = ((bf16[128,64,128]{2,1,0:T(8,128)(2,1)}), bf16[128,64,128]{2,1,0:T(8,128)(2,1)S(1)}, u32[]{:S(2)}, u32[]{:S(2)}) async-start(bf16[128,64,128]{2,1,0:T(8,128)(2,1)} %products.1), calls=%async_computation | async-start | bytes 4194304 | tf_op jit(solution)/shard_map/all_to_all | solution.py:393
  15.0 29.9 %copy-start.2 = (bf16[256,256]{1,0:T(8,128)(2,1)S(1)}, bf16[256,256]{1,0:T(8,128)(2,1)}, u32[]{:S(2)}) copy-start(bf16[256,256]{1,0:T(8,128)(2,1)} %constant.32.clone.fold) | copy-start | bytes 393220
  15.0 29.9 %copy-start.3 = (bf16[256,256]{1,0:T(8,128)(2,1)S(1)}, bf16[256,256]{1,0:T(8,128)(2,1)}, u32[]{:S(2)}) copy-start(bf16[256,256]{1,0:T(8,128)(2,1)} %constant.39.clone.gather) | copy-start | bytes 393220
  15.0 29.9 %copy-start.4 = (bf16[256,256]{1,0:T(8,128)(2,1)S(1)}, bf16[256,256]{1,0:T(8,128)(2,1)}, u32[]{:S(2)}) copy-start(bf16[256,256]{1,0:T(8,128)(2,1)} %constant.38.clone.spread) | copy-start | bytes 393220
  15.1 29.9 %copy-start.5 = (f32[128,128]{1,0:T(8,128)S(1)}, f32[128,128]{1,0:T(8,128)}, u32[]{:S(2)}) copy-start(f32[128,128]{1,0:T(8,128)} %constant.35.clone.turn_im) | copy-start | bytes 196612
  15.1 29.9 %copy-start.6 = (f32[128,128]{1,0:T(8,128)S(1)}, f32[128,128]{1,0:T(8,128)}, u32[]{:S(2)}) copy-start(f32[128,128]{1,0:T(8,128)} %constant.34.clone.turn_re) | copy-start | bytes 196612
  15.1 29.9 %copy-start.7 = (bf16[128,256]{1,0:T(8,128)(2,1)S(1)}, bf16[128,256]{1,0:T(8,128)(2,1)}, u32[]{:S(2)}) copy-start(bf16[128,256]{1,0:T(8,128)(2,1)} %constant.41.clone.unfold_lo) | copy-start | bytes 196612
  15.1 29.9 %copy-start.8 = (bf16[128,256]{1,0:T(8,128)(2,1)S(1)}, bf16[128,256]{1,0:T(8,128)(2,1)}, u32[]{:S(2)}) copy-start(bf16[128,256]{1,0:T(8,128)(2,1)} %constant.40.clone.unfold_hi) | copy-start | bytes 196612
  54.0 34.8 %all-to-all-start.1 = ((bf16[128,64,128]{2,1,0:T(8,128)(2,1)}), bf16[128,64,128]{2,1,0:T(8,128)(2,1)S(1)}, u32[]{:S(2)}, u32[]{:S(2)}) async-start(bf16[128,64,128]{2,1,0:T(8,128)(2,1)} %get-tuple-element.13), calls=%async_computation.1 | async-start | bytes 4194304 | tf_op jit(solution)/shard_map/all_to_all | solution.py:393
  59.8 29.1 %copy-start = (bf16[4096,128]{1,0:T(8,128)(2,1)S(1)}, bf16[4096,128]{1,0:T(8,128)(2,1)}, u32[]{:S(2)}) copy-start(bf16[4096,128]{1,0:T(8,128)(2,1)} %query.3) | copy-start | bytes 3145732
  59.8 29.1 %copy-start.1 = (f32[4096]{0:T(1024)S(1)}, f32[4096]{0:T(1024)}, u32[]{:S(2)}) copy-start(f32[4096]{0:T(1024)} %param.24) | copy-start | bytes 49156

commit v5 on v4

--- a/solution.py
+++ b/solution.py
@@ -347,8 +347,8 @@
     loads = fetches((key_in, value_in, cotangent), (k, v, c), in_sem)
     stores = fetches(results, (output, grad_query, grad_key, grad_value), out_sem)
     for group in loads:
-        for copy in group:
-            copy.start()
+        for j, copy in enumerate(group):
+            copy.start(priority=j % 2)
     for i in range(gain.shape[0]):
         spread[i * SIDE:(i + 1) * SIDE, :] = jnp.broadcast_to(gain[i:i + 1, :], (SIDE, SIDE)).T
     for i in range(PIECES):
@@ -362,8 +362,8 @@
         dmixed = back + g * (ci * qi).astype(BF16).astype(F32)
         for store, value in zip(results, (qi * inner, ci * inner, dmixed * vi, dmixed * ki)):
             chunk(store, i)[...] = value.astype(BF16)
-        for copy in stores[i]:
-            copy.start()
+        for j, copy in enumerate(stores[i]):
+            copy.start(priority=j % 2)
     for group in stores:
         for copy in group:
             copy.wait()

time: 93.6 us -> 94.1 us (level)
  no operation moved by 1% of the time
where the time goes in v5:
time: 94.1 us; the launch traced here: 93.7 us
  waiting for transfers between devices  46.5 us (49%)
  Pallas kernels  29.2 us (31%)
  starting transfers between devices  16.2 us (17%)
    all_to_all x2, waiting for transfers between devices, exchange(): lax.all_to_all(blocks, ('node', 'local'), split_axis=0, concat_axis=0, ti...  46.5 us
    all_to_all x2, starting transfers between devices, exchange(): lax.all_to_all(blocks, ('node', 'local'), split_axis=0, concat_axis=0, ti...  16.2 us
    pallas_call x1, Pallas kernels, convolve(): pl.pallas_call(signal_kernel, in_specs=[NEAR, FAR] + [NEAR] * len(ops), o...  9 us
    pallas_call x1, Pallas kernels, filter_spectra(): pl.pallas_call(filter_kernel, grid=(groups,), in_specs=[pl.BlockSpec((GRO...  6.65 us
    pallas_call x1, Pallas kernels, filter_gradient(): pl.pallas_call(functools.partial(grad_kernel, scale / tab['cross_gain']),...  5.7 us
    pallas_call x1, Pallas kernels, finish(): pl.pallas_call(finish_kernel, in_specs=[NEAR] + [FAR] * 3 + [NEAR] * 2, o...  4.66 us
    pallas_call x1, Pallas kernels, products(): pl.pallas_call(products_kernel, in_specs=[FAR] * 4, out_specs=FAR, out_sh...  3.23 us
  transfers between devices with their start and end apart: 2, of which 2 were waited for; matrix products, arithmetic and copies ran while one was open for 1% of the time, Pallas kernels for 13%

profile of v5, /device:TPU:0, one launch (start us, length us, event | category | flops | bytes accessed | tf_op | source)
XLA Modules:
  0.0 93.7 jit_solution(15002812284029030066)
XLA Ops:
  0.6 3.2 %products.1 = bf16[128,64,128]{2,1,0:T(8,128)(2,1)} custom-call(bf16[4096,128]{1,0:T(8,128)(2,1)} %query.3, bf16[4096,128]{1,0:T(8,128)(2,1)} %key_in.3, bf16[4096,128]{1,0:T(8,128)(2,1)} %value_in.3, bf16[4096,128]{1,0:T(8,128)(2,1)} %cotangent.3), custom_call_target="tpu_custom_call" | custom-call | flops 1048576 | bytes 6291456 | tf_op jit(solution)/shard_map/products/pallas_call | solution.py:331
  3.9 11.1 %all-to-all-start = ((bf16[128,64,128]{2,1,0:T(8,128)(2,1)}), bf16[128,64,128]{2,1,0:T(8,128)(2,1)S(1)}, u32[]{:S(2)}, u32[]{:S(2)}) async-start(bf16[128,64,128]{2,1,0:T(8,128)(2,1)} %products.1), calls=%async_computation | async-start | bytes 4194304 | tf_op jit(solution)/shard_map/all_to_all | solution.py:393
  15.0 0.0 copy-start.2
  15.0 0.0 copy-start.3
  15.0 0.0 copy-start.4
  15.1 0.0 copy-start.5
  15.1 0.0 copy-start.6
  15.1 0.0 copy-start.7
  15.1 0.0 copy-start.8
  15.1 6.6 %filter_spectra.1.fil = f32[4,8,128,256]{3,2,1,0:T(8,128)} custom-call(f32[32,16384]{1,0:T(8,128)} %fil.1, bf16[256,256]{1,0:T(8,128)(2,1)} %constant.32.clone.fold, bf16[256,128]{1,0:T(8,128)(2,1)} %constant.33.clone.fold_hi, f32[128,128]{1,0:T(8,128)} %constant.34.clone.turn_re, f32[128,128]{1,0:T(8,128)} %constant.35.clone.turn_im, ...), custom_call_target="tpu_custom_call" | custom-call | flops 2684354560 | bytes 6291456 | tf_op jit(solution)/shard_map/filter_spectra/pallas_call | solution.py:247
  21.8 23.2 %all-to-all-done.got = bf16[128,64,128]{2,1,0:T(8,128)(2,1)S(1)} async-done(((bf16[128,64,128]{2,1,0:T(8,128)(2,1)}), bf16[128,64,128]{2,1,0:T(8,128)(2,1)S(1)}, u32[]{:S(2)}, u32[]{:S(2)}) %all-to-all-start) | async-done | bytes 2097184 | tf_op jit(solution)/shard_map/all_to_all | solution.py:393
  45.0 0.0 copy-done.2
  45.0 0.0 copy-done.3
  45.0 0.0 copy-done.4
  45.0 0.0 copy-done.5
  45.0 0.0 copy-done.6
  45.0 0.0 copy-done.7
  45.0 0.0 copy-done.8
  45.0 9.0 %convolve.1 = (bf16[128,64,128]{2,1,0:T(8,128)(2,1)}, bf16[4,8,128,256]{3,2,1,0:T(8,128)(2,1)}, f32[4,8,128]{2,1,0:T(8,128)S(1)}) custom-call(bf16[128,64,128]{2,1,0:T(8,128)(2,1)S(1)} %all-to-all-done.got, f32[4,8,128,256]{3,2,1,0:T(8,128)} %filter_spectra.1.fil, bf16[256,256]{1,0:T(8,128)(2,1)S(1)} %copy-done.2, f32[128,128]{1,0:T(8,128)S(1)} %copy-done.6, ...), custom_call_target="tpu_custom_call" | custom-call | flops 9126805504 | bytes 6291456 | tf_op jit(solution)/shard_map/convolve/pallas_call | solution.py:265
  54.0 5.1 %all-to-all-start.1 = ((bf16[128,64,128]{2,1,0:T(8,128)(2,1)}), bf16[128,64,128]{2,1,0:T(8,128)(2,1)S(1)}, u32[]{:S(2)}, u32[]{:S(2)}) async-start(bf16[128,64,128]{2,1,0:T(8,128)(2,1)} %get-tuple-element.13), calls=%async_computation.1 | async-start | bytes 4194304 | tf_op jit(solution)/shard_map/all_to_all | solution.py:393
  59.1 0.1 reduce_sum.9
  59.2 0.6 mul.11
  59.8 0.0 copy-start
  59.8 0.0 copy-start.1
  59.8 5.7 %filter_gradient.1 = f32[32,16384]{1,0:T(8,128)} custom-call(bf16[4,8,128,256]{3,2,1,0:T(8,128)(2,1)} %get-tuple-element.18.cross, f32[128,128]{1,0:T(8,128)} %constant.34.clone.turn_re, f32[128,128]{1,0:T(8,128)} %constant.35.clone.turn_im, bf16[256,256]{1,0:T(8,128)(2,1)} %constant.42.clone.gather_hi, bf16[256,256]{1,0:T(8,128)(2,1)} %constant.43.clone.gather_lo, ...), custom_call_target="tpu_custom_call" | custom-call | flops 2684354560 | bytes 6291456 | tf_op jit(solution)/shard_map/filter_gradient/pallas_call | solution.py:285
  65.5 23.4 %all-to-all-done.1.got = bf16[128,64,128]{2,1,0:T(8,128)(2,1)S(1)} async-done(((bf16[128,64,128]{2,1,0:T(8,128)(2,1)}), bf16[128,64,128]{2,1,0:T(8,128)(2,1)S(1)}, u32[]{:S(2)}, u32[]{:S(2)}) %all-to-all-start.1) | async-done | bytes 2097184 | tf_op jit(solution)/shard_map/all_to_all | solution.py:393
  88.8 0.0 copy-done
  88.8 0.0 copy-done.1
  88.8 4.7 %finish.1 = (bf16[4096,128]{1,0:T(8,128)(2,1)}, bf16[4096,128]{1,0:T(8,128)(2,1)}, bf16[4096,128]{1,0:T(8,128)(2,1)}, bf16[4096,128]{1,0:T(8,128)(2,1)}) custom-call(bf16[4096,128]{1,0:T(8,128)(2,1)S(1)} %copy-done, bf16[4096,128]{1,0:T(8,128)(2,1)} %key_in.3, bf16[4096,128]{1,0:T(8,128)(2,1)} %value_in.3, bf16[4096,128]{1,0:T(8,128)(2,1)} %cotangent.3, ...), custom_call_target="tpu_custom_call" | custom-call | flops 5242880 | bytes 10485760 | tf_op jit(solution)/shard_map/finish/pallas_call | solution.py:374
  (1 shorter events, 0.0 us)
Async XLA Ops:
  3.9 41.1 %all-to-all-start = ((bf16[128,64,128]{2,1,0:T(8,128)(2,1)}), bf16[128,64,128]{2,1,0:T(8,128)(2,1)S(1)}, u32[]{:S(2)}, u32[]{:S(2)}) async-start(bf16[128,64,128]{2,1,0:T(8,128)(2,1)} %products.1), calls=%async_computation | async-start | bytes 4194304 | tf_op jit(solution)/shard_map/all_to_all | solution.py:393
  15.0 29.9 %copy-start.2 = (bf16[256,256]{1,0:T(8,128)(2,1)S(1)}, bf16[256,256]{1,0:T(8,128)(2,1)}, u32[]{:S(2)}) copy-start(bf16[256,256]{1,0:T(8,128)(2,1)} %constant.32.clone.fold) | copy-start | bytes 393220
  15.0 29.9 %copy-start.3 = (bf16[256,256]{1,0:T(8,128)(2,1)S(1)}, bf16[256,256]{1,0:T(8,128)(2,1)}, u32[]{:S(2)}) copy-start(bf16[256,256]{1,0:T(8,128)(2,1)} %constant.39.clone.gather) | copy-start | bytes 393220
  15.0 29.9 %copy-start.4 = (bf16[256,256]{1,0:T(8,128)(2,1)S(1)}, bf16[256,256]{1,0:T(8,128)(2,1)}, u32[]{:S(2)}) copy-start(bf16[256,256]{1,0:T(8,128)(2,1)} %constant.38.clone.spread) | copy-start | bytes 393220
  15.1 29.9 %copy-start.5 = (f32[128,128]{1,0:T(8,128)S(1)}, f32[128,128]{1,0:T(8,128)}, u32[]{:S(2)}) copy-start(f32[128,128]{1,0:T(8,128)} %constant.35.clone.turn_im) | copy-start | bytes 196612
  15.1 29.9 %copy-start.6 = (f32[128,128]{1,0:T(8,128)S(1)}, f32[128,128]{1,0:T(8,128)}, u32[]{:S(2)}) copy-start(f32[128,128]{1,0:T(8,128)} %constant.34.clone.turn_re) | copy-start | bytes 196612
  15.1 29.9 %copy-start.7 = (bf16[128,256]{1,0:T(8,128)(2,1)S(1)}, bf16[128,256]{1,0:T(8,128)(2,1)}, u32[]{:S(2)}) copy-start(bf16[128,256]{1,0:T(8,128)(2,1)} %constant.41.clone.unfold_lo) | copy-start | bytes 196612
  15.1 29.9 %copy-start.8 = (bf16[128,256]{1,0:T(8,128)(2,1)S(1)}, bf16[128,256]{1,0:T(8,128)(2,1)}, u32[]{:S(2)}) copy-start(bf16[128,256]{1,0:T(8,128)(2,1)} %constant.40.clone.unfold_hi) | copy-start | bytes 196612
  54.0 34.8 %all-to-all-start.1 = ((bf16[128,64,128]{2,1,0:T(8,128)(2,1)}), bf16[128,64,128]{2,1,0:T(8,128)(2,1)S(1)}, u32[]{:S(2)}, u32[]{:S(2)}) async-start(bf16[128,64,128]{2,1,0:T(8,128)(2,1)} %get-tuple-element.13), calls=%async_computation.1 | async-start | bytes 4194304 | tf_op jit(solution)/shard_map/all_to_all | solution.py:393
  59.8 29.1 %copy-start = (bf16[4096,128]{1,0:T(8,128)(2,1)S(1)}, bf16[4096,128]{1,0:T(8,128)(2,1)}, u32[]{:S(2)}) copy-start(bf16[4096,128]{1,0:T(8,128)(2,1)} %query.3) | copy-start | bytes 3145732
  59.8 29.1 %copy-start.1 = (f32[4096]{0:T(1024)S(1)}, f32[4096]{0:T(1024)}, u32[]{:S(2)}) copy-start(f32[4096]{0:T(1024)} %param.24) | copy-start | bytes 49156
